TPU v7x, 32 devices: a whole 2x2x4 slice. The times are simulated.
32 devices in a mesh: section: 4 (over y, core), expert: 8 (over z, x).
Axes of the slice: x: 2, y: 2, z: 4, core: 2. Of those that a mesh axis runs over, the one named last changes fastest.
Arguments:
- tokens_in: bfloat16 [8, 128, 2048], P(None, 'expert'), may hold values from -6 to 6
- expert_ids: int32 [4, 8, 128, 8], P('section'), may hold values from 0 to 7, as said below
- gate_values: float32 [4, 8, 128, 8], P('section', None, 'expert'), may hold values from 0.1 to 1
- expert_gate: bfloat16 [4, 8, 2048, 768], P('section', 'expert'), may hold values from -0.125 to 0.125
- expert_up: bfloat16 [4, 8, 2048, 768], P('section', 'expert'), may hold values from -0.125 to 0.125
- expert_down: bfloat16 [4, 8, 768, 2048], P('section', 'expert'), may hold values from -0.21875 to 0.21875
Outputs:
- layer_out: bfloat16 [4, 8, 128, 2048], P('section', None, 'expert')
Inputs may be any that keep to these rules, and one draw needn't show every extreme that they name: `expert_ids`: every row names 8 different experts. In each layer and micro-batch the 16 rows of one device (aligned blocks) name no expert more than 16 times, and one expert is named exactly 16 times by the rows of every device.
All inputs are finite; a program needn't handle non-finite values.
Results may differ from a plain program's by a relative error of at most 0.025.
Values may be sent and summed in bfloat16 or wider, within the bound.
No kernel may reach another device: no remote copies, remote signals or barrier semaphores. Data moves between devices by JAX's collectives and lax.ppermute only.
A program may use at most 64 MiB of HBM per device.

v0:
```python
import jax
import jax.numpy as jnp
from jax import lax
from jax.sharding import PartitionSpec as P

epsilon = 1e-06
block_rows = 64


def passed_along(block, axis, distance):
    devices = range(lax.axis_size(axis))
    route = [(i - distance, i) for i in devices if i - distance in devices]
    return lax.ppermute(block, axis, route)


def rms_normed(hidden):
    widened = hidden.astype(jnp.float32)
    inverse_rms = lax.rsqrt(jnp.mean(widened * widened, axis=-1, keepdims=True) + epsilon)
    return (widened * inverse_rms).astype(jnp.bfloat16)


def pack_rows(normed, route_ids, slot_most, experts):
    unit_count, row_count, features = normed.shape
    top_count = route_ids.shape[2]
    pairs = row_count * top_count
    flat_ids = route_ids.reshape(unit_count, pairs)
    expert_lane = jnp.arange(experts, dtype=jnp.int32)
    onehot = (flat_ids[:, :, None] == expert_lane[None, None, :]).astype(jnp.int32)
    ahead_count = jnp.cumsum(onehot, axis=1) - onehot
    place_in = jnp.sum(ahead_count * onehot, axis=2)
    unit_ids = jnp.arange(unit_count, dtype=jnp.int32)[:, None]
    target = flat_ids * (unit_count * slot_most) + unit_ids * slot_most + place_in
    owner_row = unit_ids * row_count + jnp.arange(pairs, dtype=jnp.int32)[None, :] // top_count
    source = jnp.full((experts * unit_count * slot_most,), unit_count * row_count, jnp.int32)
    source = source.at[target.reshape(-1)].set(owner_row.reshape(-1))
    padded = jnp.concatenate(
        [normed.reshape(unit_count * row_count, features), jnp.zeros((1, features), jnp.bfloat16)],
        axis=0,
    )
    return (padded[source].reshape(experts, unit_count * slot_most, features), target.reshape(-1))


def expert_rows(received, counts, slot_most, gate_matrix, up_matrix, down_matrix):
    features = received.shape[2]
    segments = counts.reshape(-1)
    segment_count = segments.shape[0]
    segment_ends = jnp.cumsum(segments)
    starts = segment_ends - segments
    live_total = segment_ends[-1]
    capacity = segment_count * slot_most
    padded_rows = -(-capacity // block_rows) * block_rows
    flat_rows = jnp.concatenate(
        [received.reshape(capacity, features), jnp.zeros((1, features), jnp.bfloat16)], axis=0
    )
    positions = jnp.arange(padded_rows, dtype=jnp.int32)
    segment = jnp.sum((segment_ends[None, :] <= positions[:, None]).astype(jnp.int32), axis=1)
    segment_clip = jnp.minimum(segment, segment_count - 1)
    offset_in = positions - starts[segment_clip]
    pick_index = jnp.where(positions < live_total, segment_clip * slot_most + offset_in, capacity)
    compact = flat_rows[pick_index]

    def one_block(block_index, finished):
        first_row = block_index * block_rows
        row_block = lax.dynamic_slice_in_dim(compact, first_row, block_rows, 0)
        gate_part = jnp.dot(row_block, gate_matrix, preferred_element_type=jnp.float32)
        up_part = jnp.dot(row_block, up_matrix, preferred_element_type=jnp.float32)
        activated = (jax.nn.silu(gate_part) * up_part).astype(jnp.bfloat16)
        result = jnp.dot(activated, down_matrix, preferred_element_type=jnp.float32).astype(
            jnp.bfloat16
        )
        return lax.dynamic_update_slice_in_dim(finished, result, first_row, 0)

    blocks = (live_total + block_rows - 1) // block_rows
    finished = lax.fori_loop(0, blocks, one_block, jnp.zeros((padded_rows, features), jnp.bfloat16))
    finished_pad = jnp.concatenate([finished, jnp.zeros((1, features), jnp.bfloat16)], axis=0)
    column = jnp.arange(slot_most, dtype=jnp.int32)
    back_index = jnp.where(
        column[None, :] < segments[:, None], starts[:, None] + column[None, :], padded_rows
    )
    return finished_pad[back_index.reshape(-1)].reshape(received.shape)


def combine_rows(hidden, returned, target, gate_rows):
    unit_count, row_count, features = hidden.shape
    top_count = gate_rows.shape[2]
    flat_back = returned.reshape(-1, features)
    picked = (
        flat_back[target].reshape(unit_count, row_count, top_count, features).astype(jnp.float32)
    )
    summed = hidden.astype(jnp.float32) + jnp.sum(gate_rows[:, :, :, None] * picked, axis=2)
    return summed.astype(jnp.bfloat16)


def body(tokens_in, expert_ids, gate_values, expert_gate, expert_up, expert_down):
    sections = lax.axis_size("section")
    section_now = lax.axis_index("section")
    experts = lax.axis_size("expert")
    my_expert = lax.axis_index("expert")
    batches, row_count, features = tokens_in.shape
    top_count = expert_ids.shape[3]
    slot_most = min(row_count, 3 * row_count * top_count // (2 * experts))
    gate_matrix = expert_gate[0, 0]
    up_matrix = expert_up[0, 0]
    down_matrix = expert_down[0, 0]
    routes_all = expert_ids[0]
    my_routes = lax.dynamic_slice_in_dim(routes_all, my_expert * row_count, row_count, 1)
    named_me = jnp.sum((routes_all == my_expert).astype(jnp.int32), axis=2)
    named_me = jnp.sum(named_me.reshape(batches, experts, row_count), axis=2)
    gates_local = gate_values[0]
    group_size = 1
    rounds = batches // group_size
    tick_count = sections + rounds - 1

    def one_tick(tick_index, loop_state):
        carried, outputs = loop_state
        round_now = tick_index - section_now
        active = (round_now >= 0) & (round_now < rounds)
        round_clip = jnp.clip(round_now, 0, rounds - 1)
        first_batch = round_clip * group_size
        fresh_rows = lax.dynamic_slice_in_dim(tokens_in, first_batch, group_size, 0)
        hidden = jnp.where(section_now == 0, fresh_rows, carried)
        routes = lax.dynamic_slice_in_dim(my_routes, first_batch, group_size, 0)
        gate_rows = lax.dynamic_slice_in_dim(gates_local, first_batch, group_size, 0)
        counts = lax.dynamic_slice_in_dim(named_me, first_batch, group_size, 0).T * active.astype(
            jnp.int32
        )
        normed = rms_normed(hidden)
        buffer, target = pack_rows(normed, routes, slot_most, experts)
        received = lax.all_to_all(buffer, "expert", split_axis=0, concat_axis=0, tiled=True)
        out_rows = expert_rows(received, counts, slot_most, gate_matrix, up_matrix, down_matrix)
        returned = lax.all_to_all(out_rows, "expert", split_axis=0, concat_axis=0, tiled=True)
        result = combine_rows(hidden, returned, target, gate_rows)
        previous = lax.dynamic_slice_in_dim(outputs, first_batch, group_size, 0)
        outputs = lax.dynamic_update_slice_in_dim(
            outputs, jnp.where(active, result, previous), first_batch, 0
        )
        carried = passed_along(result, "section", 1)
        return (carried, outputs)

    initial = (
        jnp.zeros((group_size, row_count, features), jnp.bfloat16),
        jnp.zeros((batches, row_count, features), jnp.bfloat16),
    )
    carried, outputs = lax.fori_loop(0, tick_count, one_tick, initial)
    return outputs[None]


def solution(mesh):
    return jax.shard_map(
        body,
        mesh=mesh,
        in_specs=(
            P(None, "expert", None),
            P("section", None, None, None),
            P("section", None, "expert", None),
            P("section", "expert", None, None),
            P("section", "expert", None, None),
            P("section", "expert", None, None),
        ),
        out_specs=P("section", None, "expert", None),
        check_vma=False,
    )
```

profile of v0, /device:TPU:5, one launch (start us, length us, event | category | flops | bytes accessed | tf_op | source)
XLA Modules:
  0.0 761.3 jit_solution(9225015735298108659)
XLA Ops:
  2.8 758.5 %while.64 = (s32[]{:T(128)}, bf16[1,16,2048]{2,1,0:T(8,128)(2,1)S(1)}, bf16[8,16,2048]{2,1,0:T(8,128)(2,1)}, pred[]{:T(512)}, s32[]{:T(128)}, /*index=5*/bf16[8,...) while((s32[]{:T(128)}, ...), condition=%wide.region_12.13_spmd, body=%wide.region_2.12_spmd.sunk | while | flops 605670272 | bytes 37095048 | solution.py:144
  7.7 5.5 all-to-all-start
  15.4 5.6 fusion.64
  21.0 5.7 all-to-all-done
  36.5 4.9 all-to-all-start.1
  42.1 12.7 %all-to-all-done.1 = bf16[8,16,2048]{2,1,0:T(8,128)(2,1)S(1)} async-done(((bf16[8,16,2048]{2,1,0:T(8,128)(2,1)}), bf16[8,16,2048]{2,1,0:T(8,128)(2,1)S(1)}, u32[]{:S(2)}, u32[]{:S(2)}) %all-to-all-start.1) | async-done | bytes 524320 | tf_op jit(solution)/shard_map/while/body/eval_jaxpr/all_to_all | solution.py:131
  72.8 5.6 fusion.64
  90.9 6.4 all-to-all-start.1
  98.1 10.1 %all-to-all-done.1 = bf16[8,16,2048]{2,1,0:T(8,128)(2,1)S(1)} async-done(((bf16[8,16,2048]{2,1,0:T(8,128)(2,1)}), bf16[8,16,2048]{2,1,0:T(8,128)(2,1)S(1)}, u32[]{:S(2)}, u32[]{:S(2)}) %all-to-all-start.1) | async-done | bytes 524320 | tf_op jit(solution)/shard_map/while/body/eval_jaxpr/all_to_all | solution.py:131
  112.5 5.9 collective-permute-done
  128.8 5.6 fusion.64
  145.6 4.1 all-to-all-start.1
  150.4 12.6 %all-to-all-done.1 = bf16[8,16,2048]{2,1,0:T(8,128)(2,1)S(1)} async-done(((bf16[8,16,2048]{2,1,0:T(8,128)(2,1)}), bf16[8,16,2048]{2,1,0:T(8,128)(2,1)S(1)}, u32[]{:S(2)}, u32[]{:S(2)}) %all-to-all-start.1) | async-done | bytes 524320 | tf_op jit(solution)/shard_map/while/body/eval_jaxpr/all_to_all | solution.py:131
  167.2 40.6 %collective-permute-done = bf16[1,16,2048]{2,1,0:T(8,128)(2,1)S(1)} collective-permute-done((bf16[1,16,2048]{2,1,0:T(8,128)(2,1)S(1)}, bf16[1,16,2048]{2,1,0:T(8,128)(2,1)S(1)}, u32[]{:S(2)}, u32[]{:S(2)}) %collective-permute-start) | collective-permute-done | bytes 65568 | tf_op jit(solution)/shard_map/while/body/eval_jaxpr/ppermute | solution.py:13
  218.3 5.6 fusion.64
  232.2 13.3 %while.65 = (s32[]{:T(128)}, bf16[128,2048]{1,0:T(8,128)(2,1)}, s32[]{:T(128)}, bf16[128,2048]{1,0:T(8,128)(2,1)}, bf16[2048,768]{1,0:T(8,128)(2,1)}, /*index=5*...) while((s32[]{:T(128)}, bf16[128,2048]{1,0:T(8,128)(2,1)}, ...), condition=%wide.region_10.10_spmd, body=%wide.region_9.9_spmd.sunk | while | flops 604405760 | bytes 10618015 | solution.py:74
  253.2 8.4 %all-to-all-done.1 = bf16[8,16,2048]{2,1,0:T(8,128)(2,1)S(1)} async-done(((bf16[8,16,2048]{2,1,0:T(8,128)(2,1)}), bf16[8,16,2048]{2,1,0:T(8,128)(2,1)S(1)}, u32[]{:S(2)}, u32[]{:S(2)}) %all-to-all-start.1) | async-done | bytes 524320 | tf_op jit(solution)/shard_map/while/body/eval_jaxpr/all_to_all | solution.py:131
  265.7 9.1 %collective-permute-done = bf16[1,16,2048]{2,1,0:T(8,128)(2,1)S(1)} collective-permute-done((bf16[1,16,2048]{2,1,0:T(8,128)(2,1)S(1)}, bf16[1,16,2048]{2,1,0:T(8,128)(2,1)S(1)}, u32[]{:S(2)}, u32[]{:S(2)}) %collective-permute-start) | collective-permute-done | bytes 65568 | tf_op jit(solution)/shard_map/while/body/eval_jaxpr/ppermute | solution.py:13
  285.3 5.6 fusion.64
  299.3 13.3 %while.65 = (s32[]{:T(128)}, bf16[128,2048]{1,0:T(8,128)(2,1)}, s32[]{:T(128)}, bf16[128,2048]{1,0:T(8,128)(2,1)}, bf16[2048,768]{1,0:T(8,128)(2,1)}, /*index=5*...) while((s32[]{:T(128)}, bf16[128,2048]{1,0:T(8,128)(2,1)}, ...), condition=%wide.region_10.10_spmd, body=%wide.region_9.9_spmd.sunk | while | flops 604405760 | bytes 10618015 | solution.py:74
  315.4 4.1 all-to-all-start.1
  320.3 8.4 %all-to-all-done.1 = bf16[8,16,2048]{2,1,0:T(8,128)(2,1)S(1)} async-done(((bf16[8,16,2048]{2,1,0:T(8,128)(2,1)}), bf16[8,16,2048]{2,1,0:T(8,128)(2,1)S(1)}, u32[]{:S(2)}, u32[]{:S(2)}) %all-to-all-start.1) | async-done | bytes 524320 | tf_op jit(solution)/shard_map/while/body/eval_jaxpr/all_to_all | solution.py:131
  332.8 12.8 %collective-permute-done = bf16[1,16,2048]{2,1,0:T(8,128)(2,1)S(1)} collective-permute-done((bf16[1,16,2048]{2,1,0:T(8,128)(2,1)S(1)}, bf16[1,16,2048]{2,1,0:T(8,128)(2,1)S(1)}, u32[]{:S(2)}, u32[]{:S(2)}) %collective-permute-start) | collective-permute-done | bytes 65568 | tf_op jit(solution)/shard_map/while/body/eval_jaxpr/ppermute | solution.py:13
  356.1 5.6 fusion.64
  370.0 13.3 %while.65 = (s32[]{:T(128)}, bf16[128,2048]{1,0:T(8,128)(2,1)}, s32[]{:T(128)}, bf16[128,2048]{1,0:T(8,128)(2,1)}, bf16[2048,768]{1,0:T(8,128)(2,1)}, /*index=5*...) while((s32[]{:T(128)}, bf16[128,2048]{1,0:T(8,128)(2,1)}, ...), condition=%wide.region_10.10_spmd, body=%wide.region_9.9_spmd.sunk | while | flops 604405760 | bytes 10618015 | solution.py:74
  391.0 8.4 %all-to-all-done.1 = bf16[8,16,2048]{2,1,0:T(8,128)(2,1)S(1)} async-done(((bf16[8,16,2048]{2,1,0:T(8,128)(2,1)}), bf16[8,16,2048]{2,1,0:T(8,128)(2,1)S(1)}, u32[]{:S(2)}, u32[]{:S(2)}) %all-to-all-start.1) | async-done | bytes 524320 | tf_op jit(solution)/shard_map/while/body/eval_jaxpr/all_to_all | solution.py:131
  403.6 12.8 %collective-permute-done = bf16[1,16,2048]{2,1,0:T(8,128)(2,1)S(1)} collective-permute-done((bf16[1,16,2048]{2,1,0:T(8,128)(2,1)S(1)}, bf16[1,16,2048]{2,1,0:T(8,128)(2,1)S(1)}, u32[]{:S(2)}, u32[]{:S(2)}) %collective-permute-start) | collective-permute-done | bytes 65568 | tf_op jit(solution)/shard_map/while/body/eval_jaxpr/ppermute | solution.py:13
  426.8 5.6 fusion.64
  440.8 13.3 %while.65 = (s32[]{:T(128)}, bf16[128,2048]{1,0:T(8,128)(2,1)}, s32[]{:T(128)}, bf16[128,2048]{1,0:T(8,128)(2,1)}, bf16[2048,768]{1,0:T(8,128)(2,1)}, /*index=5*...) while((s32[]{:T(128)}, bf16[128,2048]{1,0:T(8,128)(2,1)}, ...), condition=%wide.region_10.10_spmd, body=%wide.region_9.9_spmd.sunk | while | flops 604405760 | bytes 10618015 | solution.py:74
  461.8 8.4 %all-to-all-done.1 = bf16[8,16,2048]{2,1,0:T(8,128)(2,1)S(1)} async-done(((bf16[8,16,2048]{2,1,0:T(8,128)(2,1)}), bf16[8,16,2048]{2,1,0:T(8,128)(2,1)S(1)}, u32[]{:S(2)}, u32[]{:S(2)}) %all-to-all-start.1) | async-done | bytes 524320 | tf_op jit(solution)/shard_map/while/body/eval_jaxpr/all_to_all | solution.py:131
  474.3 12.8 %collective-permute-done = bf16[1,16,2048]{2,1,0:T(8,128)(2,1)S(1)} collective-permute-done((bf16[1,16,2048]{2,1,0:T(8,128)(2,1)S(1)}, bf16[1,16,2048]{2,1,0:T(8,128)(2,1)S(1)}, u32[]{:S(2)}, u32[]{:S(2)}) %collective-permute-start) | collective-permute-done | bytes 65568 | tf_op jit(solution)/shard_map/while/body/eval_jaxpr/ppermute | solution.py:13
  497.6 5.6 fusion.64
  511.5 13.3 %while.65 = (s32[]{:T(128)}, bf16[128,2048]{1,0:T(8,128)(2,1)}, s32[]{:T(128)}, bf16[128,2048]{1,0:T(8,128)(2,1)}, bf16[2048,768]{1,0:T(8,128)(2,1)}, /*index=5*...) while((s32[]{:T(128)}, bf16[128,2048]{1,0:T(8,128)(2,1)}, ...), condition=%wide.region_10.10_spmd, body=%wide.region_9.9_spmd.sunk | while | flops 604405760 | bytes 10618015 | solution.py:74
  532.5 8.4 %all-to-all-done.1 = bf16[8,16,2048]{2,1,0:T(8,128)(2,1)S(1)} async-done(((bf16[8,16,2048]{2,1,0:T(8,128)(2,1)}), bf16[8,16,2048]{2,1,0:T(8,128)(2,1)S(1)}, u32[]{:S(2)}, u32[]{:S(2)}) %all-to-all-start.1) | async-done | bytes 524320 | tf_op jit(solution)/shard_map/while/body/eval_jaxpr/all_to_all | solution.py:131
  545.0 12.8 %collective-permute-done = bf16[1,16,2048]{2,1,0:T(8,128)(2,1)S(1)} collective-permute-done((bf16[1,16,2048]{2,1,0:T(8,128)(2,1)S(1)}, bf16[1,16,2048]{2,1,0:T(8,128)(2,1)S(1)}, u32[]{:S(2)}, u32[]{:S(2)}) %collective-permute-start) | collective-permute-done | bytes 65568 | tf_op jit(solution)/shard_map/while/body/eval_jaxpr/ppermute | solution.py:13
  568.3 5.6 fusion.64
  582.2 13.3 %while.65 = (s32[]{:T(128)}, bf16[128,2048]{1,0:T(8,128)(2,1)}, s32[]{:T(128)}, bf16[128,2048]{1,0:T(8,128)(2,1)}, bf16[2048,768]{1,0:T(8,128)(2,1)}, /*index=5*...) while((s32[]{:T(128)}, bf16[128,2048]{1,0:T(8,128)(2,1)}, ...), condition=%wide.region_10.10_spmd, body=%wide.region_9.9_spmd.sunk | while | flops 604405760 | bytes 10618015 | solution.py:74
  603.2 8.4 %all-to-all-done.1 = bf16[8,16,2048]{2,1,0:T(8,128)(2,1)S(1)} async-done(((bf16[8,16,2048]{2,1,0:T(8,128)(2,1)}), bf16[8,16,2048]{2,1,0:T(8,128)(2,1)S(1)}, u32[]{:S(2)}, u32[]{:S(2)}) %all-to-all-start.1) | async-done | bytes 524320 | tf_op jit(solution)/shard_map/while/body/eval_jaxpr/all_to_all | solution.py:131
  615.8 12.8 %collective-permute-done = bf16[1,16,2048]{2,1,0:T(8,128)(2,1)S(1)} collective-permute-done((bf16[1,16,2048]{2,1,0:T(8,128)(2,1)S(1)}, bf16[1,16,2048]{2,1,0:T(8,128)(2,1)S(1)}, u32[]{:S(2)}, u32[]{:S(2)}) %collective-permute-start) | collective-permute-done | bytes 65568 | tf_op jit(solution)/shard_map/while/body/eval_jaxpr/ppermute | solution.py:13
  639.1 5.6 fusion.64
  653.3 13.3 %while.65 = (s32[]{:T(128)}, bf16[128,2048]{1,0:T(8,128)(2,1)}, s32[]{:T(128)}, bf16[128,2048]{1,0:T(8,128)(2,1)}, bf16[2048,768]{1,0:T(8,128)(2,1)}, /*index=5*...) while((s32[]{:T(128)}, bf16[128,2048]{1,0:T(8,128)(2,1)}, ...), condition=%wide.region_10.10_spmd, body=%wide.region_9.9_spmd.sunk | while | flops 604405760 | bytes 10618015 | solution.py:74
  669.5 7.4 all-to-all-start.1
  677.7 10.1 %all-to-all-done.1 = bf16[8,16,2048]{2,1,0:T(8,128)(2,1)S(1)} async-done(((bf16[8,16,2048]{2,1,0:T(8,128)(2,1)}), bf16[8,16,2048]{2,1,0:T(8,128)(2,1)S(1)}, u32[]{:S(2)}, u32[]{:S(2)}) %all-to-all-start.1) | async-done | bytes 524320 | tf_op jit(solution)/shard_map/while/body/eval_jaxpr/all_to_all | solution.py:131
  692.0 5.9 collective-permute-done
  708.4 5.6 fusion.64
  723.6 13.3 %while.65 = (s32[]{:T(128)}, bf16[128,2048]{1,0:T(8,128)(2,1)}, s32[]{:T(128)}, bf16[128,2048]{1,0:T(8,128)(2,1)}, bf16[2048,768]{1,0:T(8,128)(2,1)}, /*index=5*...) while((s32[]{:T(128)}, bf16[128,2048]{1,0:T(8,128)(2,1)}, ...), condition=%wide.region_10.10_spmd, body=%wide.region_9.9_spmd.sunk | while | flops 604405760 | bytes 10618015 | solution.py:74
  739.7 6.4 all-to-all-start.1
  747.0 8.4 %all-to-all-done.1 = bf16[8,16,2048]{2,1,0:T(8,128)(2,1)S(1)} async-done(((bf16[8,16,2048]{2,1,0:T(8,128)(2,1)}), bf16[8,16,2048]{2,1,0:T(8,128)(2,1)S(1)}, u32[]{:S(2)}, u32[]{:S(2)}) %all-to-all-start.1) | async-done | bytes 524320 | tf_op jit(solution)/shard_map/while/body/eval_jaxpr/all_to_all | solution.py:131
  (542 shorter events, 416.3 us)
Async XLA Ops:
  7.7 19.0 %all-to-all-start = ((bf16[8,16,2048]{2,1,0:T(8,128)(2,1)}), bf16[8,16,2048]{2,1,0:T(8,128)(2,1)S(1)}, u32[]{:S(2)}, u32[]{:S(2)}) async-start(bf16[8,16,2048]{2,1,0:T(8,128)(2,1)} %bitcast.140), calls=%async_computation | async-start | bytes 1048576 | tf_op jit(solution)/shard_map/while/body/eval_jaxpr/all_to_all | solution.py:129
  26.7 0.8 copy-start.1
  27.5 6.2 copy-start
  36.5 18.4 %all-to-all-start.1 = ((bf16[8,16,2048]{2,1,0:T(8,128)(2,1)}), bf16[8,16,2048]{2,1,0:T(8,128)(2,1)S(1)}, u32[]{:S(2)}, u32[]{:S(2)}) async-start(bf16[8,16,2048]{2,1,0:T(8,128)(2,1)} %bitcast.151), calls=%async_computation.1 | async-start | bytes 1048576 | tf_op jit(solution)/shard_map/while/body/eval_jaxpr/all_to_all | solution.py:131
  57.8 4.6 collective-permute-start
  67.2 13.9 %all-to-all-start = ((bf16[8,16,2048]{2,1,0:T(8,128)(2,1)}), bf16[8,16,2048]{2,1,0:T(8,128)(2,1)S(1)}, u32[]{:S(2)}, u32[]{:S(2)}) async-start(bf16[8,16,2048]{2,1,0:T(8,128)(2,1)} %bitcast.140), calls=%async_computation | async-start | bytes 1048576 | tf_op jit(solution)/shard_map/while/body/eval_jaxpr/all_to_all | solution.py:129
  81.1 0.8 copy-start.1
  81.9 6.2 copy-start
  90.9 17.4 %all-to-all-start.1 = ((bf16[8,16,2048]{2,1,0:T(8,128)(2,1)}), bf16[8,16,2048]{2,1,0:T(8,128)(2,1)S(1)}, u32[]{:S(2)}, u32[]{:S(2)}) async-start(bf16[8,16,2048]{2,1,0:T(8,128)(2,1)} %bitcast.151), calls=%async_computation.1 | async-start | bytes 1048576 | tf_op jit(solution)/shard_map/while/body/eval_jaxpr/all_to_all | solution.py:131
  111.2 7.2 collective-permute-start
  123.2 12.6 %all-to-all-start = ((bf16[8,16,2048]{2,1,0:T(8,128)(2,1)}), bf16[8,16,2048]{2,1,0:T(8,128)(2,1)S(1)}, u32[]{:S(2)}, u32[]{:S(2)}) async-start(bf16[8,16,2048]{2,1,0:T(8,128)(2,1)} %bitcast.140), calls=%async_computation | async-start | bytes 1048576 | tf_op jit(solution)/shard_map/while/body/eval_jaxpr/all_to_all | solution.py:129
  136.5 6.2 copy-start
  145.6 17.4 %all-to-all-start.1 = ((bf16[8,16,2048]{2,1,0:T(8,128)(2,1)}), bf16[8,16,2048]{2,1,0:T(8,128)(2,1)S(1)}, u32[]{:S(2)}, u32[]{:S(2)}) async-start(bf16[8,16,2048]{2,1,0:T(8,128)(2,1)} %bitcast.151), calls=%async_computation.1 | async-start | bytes 1048576 | tf_op jit(solution)/shard_map/while/body/eval_jaxpr/all_to_all | solution.py:131
  165.9 41.9 %collective-permute-start = (bf16[1,16,2048]{2,1,0:T(8,128)(2,1)S(1)}, bf16[1,16,2048]{2,1,0:T(8,128)(2,1)S(1)}, u32[]{:S(2)}, u32[]{:S(2)}) collective-permute-start(bf16[1,16,2048]{2,1,0:T(8,128)(2,1)S(1)} %get-tuple-element.648), channel_id=1, source_target_pairs={{0,8},{8,16},{16,24},{1,9},{9,17},{17,25},{2,10},{10,18},{18,26},{... | collective-permute-start | bytes 196616 | tf_op jit(solution)/shard_map/while/body/eval_jaxpr/ppermute | solution.py:13
  212.6 12.6 %all-to-all-start = ((bf16[8,16,2048]{2,1,0:T(8,128)(2,1)}), bf16[8,16,2048]{2,1,0:T(8,128)(2,1)S(1)}, u32[]{:S(2)}, u32[]{:S(2)}) async-start(bf16[8,16,2048]{2,1,0:T(8,128)(2,1)} %bitcast.140), calls=%async_computation | async-start | bytes 1048576 | tf_op jit(solution)/shard_map/while/body/eval_jaxpr/all_to_all | solution.py:129
  225.2 0.8 copy-start.1
  226.0 6.2 copy-start
  248.3 13.2 %all-to-all-start.1 = ((bf16[8,16,2048]{2,1,0:T(8,128)(2,1)}), bf16[8,16,2048]{2,1,0:T(8,128)(2,1)S(1)}, u32[]{:S(2)}, u32[]{:S(2)}) async-start(bf16[8,16,2048]{2,1,0:T(8,128)(2,1)} %bitcast.151), calls=%async_computation.1 | async-start | bytes 1048576 | tf_op jit(solution)/shard_map/while/body/eval_jaxpr/all_to_all | solution.py:131
  264.4 10.4 %collective-permute-start = (bf16[1,16,2048]{2,1,0:T(8,128)(2,1)S(1)}, bf16[1,16,2048]{2,1,0:T(8,128)(2,1)S(1)}, u32[]{:S(2)}, u32[]{:S(2)}) collective-permute-start(bf16[1,16,2048]{2,1,0:T(8,128)(2,1)S(1)} %get-tuple-element.648), channel_id=1, source_target_pairs={{0,8},{8,16},{16,24},{1,9},{9,17},{17,25},{2,10},{10,18},{18,26},{... | collective-permute-start | bytes 196616 | tf_op jit(solution)/shard_map/while/body/eval_jaxpr/ppermute | solution.py:13
  279.7 12.6 %all-to-all-start = ((bf16[8,16,2048]{2,1,0:T(8,128)(2,1)}), bf16[8,16,2048]{2,1,0:T(8,128)(2,1)S(1)}, u32[]{:S(2)}, u32[]{:S(2)}) async-start(bf16[8,16,2048]{2,1,0:T(8,128)(2,1)} %bitcast.140), calls=%async_computation | async-start | bytes 1048576 | tf_op jit(solution)/shard_map/while/body/eval_jaxpr/all_to_all | solution.py:129
  293.0 6.2 copy-start
  315.4 13.2 %all-to-all-start.1 = ((bf16[8,16,2048]{2,1,0:T(8,128)(2,1)}), bf16[8,16,2048]{2,1,0:T(8,128)(2,1)S(1)}, u32[]{:S(2)}, u32[]{:S(2)}) async-start(bf16[8,16,2048]{2,1,0:T(8,128)(2,1)} %bitcast.151), calls=%async_computation.1 | async-start | bytes 1048576 | tf_op jit(solution)/shard_map/while/body/eval_jaxpr/all_to_all | solution.py:131
  331.5 14.1 %collective-permute-start = (bf16[1,16,2048]{2,1,0:T(8,128)(2,1)S(1)}, bf16[1,16,2048]{2,1,0:T(8,128)(2,1)S(1)}, u32[]{:S(2)}, u32[]{:S(2)}) collective-permute-start(bf16[1,16,2048]{2,1,0:T(8,128)(2,1)S(1)} %get-tuple-element.648), channel_id=1, source_target_pairs={{0,8},{8,16},{16,24},{1,9},{9,17},{17,25},{2,10},{10,18},{18,26},{... | collective-permute-start | bytes 196616 | tf_op jit(solution)/shard_map/while/body/eval_jaxpr/ppermute | solution.py:13
  350.4 12.6 %all-to-all-start = ((bf16[8,16,2048]{2,1,0:T(8,128)(2,1)}), bf16[8,16,2048]{2,1,0:T(8,128)(2,1)S(1)}, u32[]{:S(2)}, u32[]{:S(2)}) async-start(bf16[8,16,2048]{2,1,0:T(8,128)(2,1)} %bitcast.140), calls=%async_computation | async-start | bytes 1048576 | tf_op jit(solution)/shard_map/while/body/eval_jaxpr/all_to_all | solution.py:129
  363.0 0.8 copy-start.1
  363.8 6.2 copy-start
  386.1 13.2 %all-to-all-start.1 = ((bf16[8,16,2048]{2,1,0:T(8,128)(2,1)}), bf16[8,16,2048]{2,1,0:T(8,128)(2,1)S(1)}, u32[]{:S(2)}, u32[]{:S(2)}) async-start(bf16[8,16,2048]{2,1,0:T(8,128)(2,1)} %bitcast.151), calls=%async_computation.1 | async-start | bytes 1048576 | tf_op jit(solution)/shard_map/while/body/eval_jaxpr/all_to_all | solution.py:131
  402.3 14.1 %collective-permute-start = (bf16[1,16,2048]{2,1,0:T(8,128)(2,1)S(1)}, bf16[1,16,2048]{2,1,0:T(8,128)(2,1)S(1)}, u32[]{:S(2)}, u32[]{:S(2)}) collective-permute-start(bf16[1,16,2048]{2,1,0:T(8,128)(2,1)S(1)} %get-tuple-element.648), channel_id=1, source_target_pairs={{0,8},{8,16},{16,24},{1,9},{9,17},{17,25},{2,10},{10,18},{18,26},{... | collective-permute-start | bytes 196616 | tf_op jit(solution)/shard_map/while/body/eval_jaxpr/ppermute | solution.py:13
  421.2 12.6 %all-to-all-start = ((bf16[8,16,2048]{2,1,0:T(8,128)(2,1)}), bf16[8,16,2048]{2,1,0:T(8,128)(2,1)S(1)}, u32[]{:S(2)}, u32[]{:S(2)}) async-start(bf16[8,16,2048]{2,1,0:T(8,128)(2,1)} %bitcast.140), calls=%async_computation | async-start | bytes 1048576 | tf_op jit(solution)/shard_map/while/body/eval_jaxpr/all_to_all | solution.py:129
  434.5 6.2 copy-start
  456.9 13.2 %all-to-all-start.1 = ((bf16[8,16,2048]{2,1,0:T(8,128)(2,1)}), bf16[8,16,2048]{2,1,0:T(8,128)(2,1)S(1)}, u32[]{:S(2)}, u32[]{:S(2)}) async-start(bf16[8,16,2048]{2,1,0:T(8,128)(2,1)} %bitcast.151), calls=%async_computation.1 | async-start | bytes 1048576 | tf_op jit(solution)/shard_map/while/body/eval_jaxpr/all_to_all | solution.py:131
  473.0 14.1 %collective-permute-start = (bf16[1,16,2048]{2,1,0:T(8,128)(2,1)S(1)}, bf16[1,16,2048]{2,1,0:T(8,128)(2,1)S(1)}, u32[]{:S(2)}, u32[]{:S(2)}) collective-permute-start(bf16[1,16,2048]{2,1,0:T(8,128)(2,1)S(1)} %get-tuple-element.648), channel_id=1, source_target_pairs={{0,8},{8,16},{16,24},{1,9},{9,17},{17,25},{2,10},{10,18},{18,26},{... | collective-permute-start | bytes 196616 | tf_op jit(solution)/shard_map/while/body/eval_jaxpr/ppermute | solution.py:13
  491.9 12.6 %all-to-all-start = ((bf16[8,16,2048]{2,1,0:T(8,128)(2,1)}), bf16[8,16,2048]{2,1,0:T(8,128)(2,1)S(1)}, u32[]{:S(2)}, u32[]{:S(2)}) async-start(bf16[8,16,2048]{2,1,0:T(8,128)(2,1)} %bitcast.140), calls=%async_computation | async-start | bytes 1048576 | tf_op jit(solution)/shard_map/while/body/eval_jaxpr/all_to_all | solution.py:129
  505.3 6.2 copy-start
  527.6 13.2 %all-to-all-start.1 = ((bf16[8,16,2048]{2,1,0:T(8,128)(2,1)}), bf16[8,16,2048]{2,1,0:T(8,128)(2,1)S(1)}, u32[]{:S(2)}, u32[]{:S(2)}) async-start(bf16[8,16,2048]{2,1,0:T(8,128)(2,1)} %bitcast.151), calls=%async_computation.1 | async-start | bytes 1048576 | tf_op jit(solution)/shard_map/while/body/eval_jaxpr/all_to_all | solution.py:131
  543.8 14.1 %collective-permute-start = (bf16[1,16,2048]{2,1,0:T(8,128)(2,1)S(1)}, bf16[1,16,2048]{2,1,0:T(8,128)(2,1)S(1)}, u32[]{:S(2)}, u32[]{:S(2)}) collective-permute-start(bf16[1,16,2048]{2,1,0:T(8,128)(2,1)S(1)} %get-tuple-element.648), channel_id=1, source_target_pairs={{0,8},{8,16},{16,24},{1,9},{9,17},{17,25},{2,10},{10,18},{18,26},{... | collective-permute-start | bytes 196616 | tf_op jit(solution)/shard_map/while/body/eval_jaxpr/ppermute | solution.py:13
  562.7 12.6 %all-to-all-start = ((bf16[8,16,2048]{2,1,0:T(8,128)(2,1)}), bf16[8,16,2048]{2,1,0:T(8,128)(2,1)S(1)}, u32[]{:S(2)}, u32[]{:S(2)}) async-start(bf16[8,16,2048]{2,1,0:T(8,128)(2,1)} %bitcast.140), calls=%async_computation | async-start | bytes 1048576 | tf_op jit(solution)/shard_map/while/body/eval_jaxpr/all_to_all | solution.py:129
  576.0 6.2 copy-start
  598.4 13.2 %all-to-all-start.1 = ((bf16[8,16,2048]{2,1,0:T(8,128)(2,1)}), bf16[8,16,2048]{2,1,0:T(8,128)(2,1)S(1)}, u32[]{:S(2)}, u32[]{:S(2)}) async-start(bf16[8,16,2048]{2,1,0:T(8,128)(2,1)} %bitcast.151), calls=%async_computation.1 | async-start | bytes 1048576 | tf_op jit(solution)/shard_map/while/body/eval_jaxpr/all_to_all | solution.py:131
  614.5 14.1 %collective-permute-start = (bf16[1,16,2048]{2,1,0:T(8,128)(2,1)S(1)}, bf16[1,16,2048]{2,1,0:T(8,128)(2,1)S(1)}, u32[]{:S(2)}, u32[]{:S(2)}) collective-permute-start(bf16[1,16,2048]{2,1,0:T(8,128)(2,1)S(1)} %get-tuple-element.648), channel_id=1, source_target_pairs={{0,8},{8,16},{16,24},{1,9},{9,17},{17,25},{2,10},{10,18},{18,26},{... | collective-permute-start | bytes 196616 | tf_op jit(solution)/shard_map/while/body/eval_jaxpr/ppermute | solution.py:13
  633.4 12.9 %all-to-all-start = ((bf16[8,16,2048]{2,1,0:T(8,128)(2,1)}), bf16[8,16,2048]{2,1,0:T(8,128)(2,1)S(1)}, u32[]{:S(2)}, u32[]{:S(2)}) async-start(bf16[8,16,2048]{2,1,0:T(8,128)(2,1)} %bitcast.140), calls=%async_computation | async-start | bytes 1048576 | tf_op jit(solution)/shard_map/while/body/eval_jaxpr/all_to_all | solution.py:129
  647.1 6.2 copy-start
  669.5 18.4 %all-to-all-start.1 = ((bf16[8,16,2048]{2,1,0:T(8,128)(2,1)}), bf16[8,16,2048]{2,1,0:T(8,128)(2,1)S(1)}, u32[]{:S(2)}, u32[]{:S(2)}) async-start(bf16[8,16,2048]{2,1,0:T(8,128)(2,1)} %bitcast.151), calls=%async_computation.1 | async-start | bytes 1048576 | tf_op jit(solution)/shard_map/while/body/eval_jaxpr/all_to_all | solution.py:131
  690.7 7.2 collective-permute-start
  702.7 13.9 %all-to-all-start = ((bf16[8,16,2048]{2,1,0:T(8,128)(2,1)}), bf16[8,16,2048]{2,1,0:T(8,128)(2,1)S(1)}, u32[]{:S(2)}, u32[]{:S(2)}) async-start(bf16[8,16,2048]{2,1,0:T(8,128)(2,1)} %bitcast.140), calls=%async_computation | async-start | bytes 1048576 | tf_op jit(solution)/shard_map/while/body/eval_jaxpr/all_to_all | solution.py:129
  717.4 6.2 copy-start
  739.7 15.6 %all-to-all-start.1 = ((bf16[8,16,2048]{2,1,0:T(8,128)(2,1)}), bf16[8,16,2048]{2,1,0:T(8,128)(2,1)S(1)}, u32[]{:S(2)}, u32[]{:S(2)}) async-start(bf16[8,16,2048]{2,1,0:T(8,128)(2,1)} %bitcast.151), calls=%async_computation.1 | async-start | bytes 1048576 | tf_op jit(solution)/shard_map/while/body/eval_jaxpr/all_to_all | solution.py:131
  758.2 3.1 collective-permute-start
  (7 other events, 5.5 us)
where the time goes:
time: 767 us; the launch traced here: 761 us
  waiting for transfers between devices  256 us (33%)
  local copies, waits for them, and re-layouts  176 us (23%)
  starting transfers between devices  108 us (14%)
  matrix products  106 us (14%)
  other arithmetic  105 us (14%)
  loops' own time  9.48 us (1%)
    ppermute x11, waiting for transfers between devices, passed_along(): return lax.ppermute(block, axis, route)  130 us
    all_to_all x11, waiting for transfers between devices, one_tick(): lax.all_to_all(out_rows, 'expert', split_axis=0, concat_axis=0, tiled=True)  104 us
    dot_general x16, matrix products, one_block(): jnp.dot(activated, down_matrix, preferred_element_type=jnp.float32)  64.6 us
    select_n x11, other arithmetic, expert_rows(): compact = flat_rows[pick_index]  61.6 us
    all_to_all x11, starting transfers between devices, one_tick(): lax.all_to_all(out_rows, 'expert', split_axis=0, concat_axis=0, tiled=True)  53.9 us
    dot_general x16, matrix products, one_block(): jnp.dot(row_block, gate_matrix, preferred_element_type=jnp.float32)  41.8 us
    all_to_all x11, starting transfers between devices, one_tick(): lax.all_to_all(buffer, 'expert', split_axis=0, concat_axis=0, tiled=True)  40.4 us
    gather x11, local copies, waits for them, and re-layouts, expert_rows(): compact = flat_rows[pick_index]  36.9 us
  transfers between devices with their start and end apart: 33, of which 33 were waited for; matrix products, arithmetic and copies ran while one was open for 11% of the time, Pallas kernels for 0%

commit v1 on v0

v1 whole, which is shorter than its diff:
```python
import functools

import jax
import jax.numpy as jnp
from jax import lax
from jax.experimental import pallas as pl
from jax.experimental.pallas import tpu as pltpu
from jax.sharding import PartitionSpec as P

epsilon = 1e-06
hidden_tile = 256


def mlp_kernel(own_ref, other_ref, weight_ref, gate_ref, up_ref, down_ref, keep_ref, give_ref, normed_ref, total_ref):
    step = pl.program_id(0)
    half = own_ref.shape[0]

    @pl.when(step == 0)
    def _():
        for place, rows_ref in enumerate((own_ref, other_ref)):
            widened = rows_ref[...].astype(jnp.float32)
            inverse_rms = lax.rsqrt(jnp.mean(widened * widened, axis=-1, keepdims=True) + epsilon)
            normed_ref[place * half : (place + 1) * half, :] = (widened * inverse_rms).astype(jnp.bfloat16)

    normed = normed_ref[...]
    gate_part = jnp.dot(normed, gate_ref[...], preferred_element_type=jnp.float32)
    up_part = jnp.dot(normed, up_ref[...], preferred_element_type=jnp.float32)
    activated = (gate_part / (1.0 + jnp.exp(-gate_part)) * up_part).astype(jnp.bfloat16)
    partial = jnp.dot(activated, down_ref[...], preferred_element_type=jnp.float32)

    @pl.when(step == 0)
    def _():
        total_ref[...] = partial

    @pl.when(step > 0)
    def _():
        total_ref[...] += partial

    @pl.when(step == pl.num_programs(0) - 1)
    def _():
        weighted = total_ref[...] * weight_ref[...]
        keep_ref[...] = weighted[:half].astype(jnp.bfloat16)
        give_ref[...] = weighted[half:].astype(jnp.bfloat16)


def expert_mlp(own, other, weights, gate_matrix, up_matrix, down_matrix):
    half, features = own.shape
    rows = 2 * half
    hidden = gate_matrix.shape[1]
    whole = lambda j: (0, 0)
    return pl.pallas_call(
        mlp_kernel,
        grid=(hidden // hidden_tile,),
        in_specs=[
            pl.BlockSpec((half, features), whole),
            pl.BlockSpec((half, features), whole),
            pl.BlockSpec((rows, 1), whole),
            pl.BlockSpec((features, hidden_tile), lambda j: (0, j)),
            pl.BlockSpec((features, hidden_tile), lambda j: (0, j)),
            pl.BlockSpec((hidden_tile, features), lambda j: (j, 0)),
        ],
        out_specs=[pl.BlockSpec((half, features), whole), pl.BlockSpec((half, features), whole)],
        out_shape=[jax.ShapeDtypeStruct((half, features), jnp.bfloat16)] * 2,
        scratch_shapes=[pltpu.VMEM((rows, features), jnp.bfloat16), pltpu.VMEM((rows, features), jnp.float32)],
        compiler_params=pltpu.CompilerParams(vmem_limit_bytes=40 * 1024 * 1024),
        cost_estimate=pl.CostEstimate(
            flops=6 * rows * features * hidden, bytes_accessed=6 * features * hidden, transcendentals=rows * hidden
        ),
        name="expert_mlp",
    )(own, other, weights, gate_matrix, up_matrix, down_matrix)


def body(tokens_in, expert_ids, gate_values, expert_gate, expert_up, expert_down):
    sections = lax.axis_size("section")
    section_now = lax.axis_index("section")
    experts = lax.axis_size("expert")
    my_expert = lax.axis_index("expert")
    columns = experts // 2
    my_column, my_side = my_expert // 2, my_expert % 2
    batches, row_count, features = tokens_in.shape
    gate_matrix, up_matrix, down_matrix = expert_gate[0, 0], expert_up[0, 0], expert_down[0, 0]
    half = columns * row_count

    my_routes = lax.dynamic_slice_in_dim(expert_ids[0], my_expert * row_count, row_count, 1)
    named = my_routes[None] == jnp.arange(experts, dtype=jnp.int32)[:, None, None, None]
    token_weights = jnp.sum(jnp.where(named, gate_values[0][None], 0.0), axis=3)
    token_weights = lax.all_to_all(token_weights, "expert", split_axis=0, concat_axis=0, tiled=True)
    apart = jnp.arange(columns, dtype=jnp.int32)
    sources = (my_column - apart) % columns * 2
    order = jnp.concatenate([sources + my_side, sources + 1 - my_side])
    token_weights = token_weights[order].transpose(1, 0, 2).reshape(batches, 2 * half, 1)

    def along_columns(block, apart, active, source_step):
        route = []
        for section in active:
            for column in range(columns):
                for side in range(2):
                    source = (section - source_step) % sections * experts + column * 2 + side
                    route.append((source, section * experts + (column + apart) % columns * 2 + side))
        return lax.ppermute(block, ("section", "expert"), route)

    def across(block, active):
        route = [(s * experts + e, s * experts + (e ^ 1)) for s in active for e in range(experts)]
        return lax.ppermute(block, ("section", "expert"), route)

    def added(*terms):
        return functools.reduce(jnp.add, [term.astype(jnp.float32) for term in terms])

    slots = 2 * sections + batches - 1
    results = []
    result = None
    second_half = None
    for slot in range(slots):
        opening = [s for s in range(sections) if 0 <= slot - 2 * s < batches]
        closing = [s for s in range(sections) if 0 <= slot - 2 * s - 1 < batches]
        if opening:
            fresh = tokens_in[min(slot, batches - 1)]
            payload = fresh if result is None else jnp.where(section_now == sections - 1, fresh, result)
            gathered = [along_columns(payload, d, opening, 1) for d in range(columns)]
        if closing:
            residual, keep, give = second_half
            received = across(give, closing)
            summed = added(keep, received).astype(jnp.bfloat16).reshape(columns, row_count, features)
            returned = [along_columns(summed[d], -d, closing, 0) for d in range(1, columns)]
            result = added(residual, summed[0], *returned).astype(jnp.bfloat16)
            results.append(result)
        if opening:
            own = jnp.concatenate(gathered, axis=0)
            other = across(own, opening)
            round_now = jnp.clip(slot - 2 * section_now, 0, batches - 1)
            weights = lax.dynamic_index_in_dim(token_weights, round_now, 0, keepdims=False)
            keep, give = expert_mlp(own, other, weights, gate_matrix, up_matrix, down_matrix)
            second_half = (gathered[0], keep, give)
    outputs = lax.dynamic_slice_in_dim(jnp.stack(results), 2 * section_now, batches, 0)
    return outputs[None]


def solution(mesh):
    return jax.shard_map(
        body,
        mesh=mesh,
        in_specs=(
            P(None, "expert", None),
            P("section", None, None, None),
            P("section", None, "expert", None),
            P("section", "expert", None, None),
            P("section", "expert", None, None),
            P("section", "expert", None, None),
        ),
        out_specs=P("section", None, "expert", None),
        check_vma=False,
    )
```

time: 767 us -> 771 us (level)
  starting transfers between devices: 108 us -> 530 us
  waiting for transfers between devices: 256 us -> 115 us
  local copies, waits for them, and re-layouts: 176 us -> 52 us
  matrix products: 106 us -> 0 us
  other arithmetic: 105 us -> 17.7 us
  Pallas kernels: 0 us -> 50.2 us
  loops' own time: 9.48 us -> 0 us
    ppermute x11 -> x126, starting transfers between devices: 14.1 us -> 527 us  [the longest x98 474 us: along_columns(): return lax.ppermute(block, ('section', 'expert'), route)]
    all_to_all x22 -> x1, waiting for transfers between devices: 126 us -> 3.65 us  [body(): lax.all_to_all(token_weights, 'expert', split_axis=0, concat_axis=0, tile...]
    dot_general x32 -> x0, matrix products: 106 us -> none  [the longest x16 64.6 us: one_block(): jnp.dot(activated, down_matrix, preferred_element_type=jnp.float32)]
    gather x55 -> x1, local copies, waits for them, and re-layouts: 92.5 us -> 0.56 us  [body(): token_weights[order].transpose(1, 0, 2).reshape(batches, 2 * half, 1)]
    all_to_all x22 -> x1, starting transfers between devices: 94.3 us -> 2.71 us  [body(): lax.all_to_all(token_weights, 'expert', split_axis=0, concat_axis=0, tile...]
    pallas_call x0 -> x14, Pallas kernels: none -> 50.2 us  [expert_mlp(): pl.pallas_call(mlp_kernel, grid=(hidden // hidden_tile,), in_specs=[pl.Bl...]
    select_n x55 -> x11, other arithmetic: 62.6 us -> 13.2 us  [the longest x10 13.1 us: body(): jnp.where(section_now == sections - 1, fresh, result)]
    unnamed x0 -> x142, local copies, waits for them, and re-layouts: none -> 42.7 us
  transfers between devices with their start and end apart: 33 -> 127, of which waited for: 33 -> 35; matrix products, arithmetic and copies ran while one was open for 11% -> 3% of each run, Pallas kernels for 0% -> 4%
where the time goes in v1:
time: 771 us; the launch traced here: 767 us
  starting transfers between devices  530 us (69%)
  waiting for transfers between devices  115 us (15%)
  local copies, waits for them, and re-layouts  52 us (7%)
  Pallas kernels  50.2 us (7%)
  other arithmetic  17.7 us (2%)
    ppermute x98, starting transfers between devices, along_columns(): return lax.ppermute(block, ('section', 'expert'), route)  474 us
    ppermute x28, waiting for transfers between devices, across(): return lax.ppermute(block, ('section', 'expert'), route)  55.7 us
    ppermute x98, waiting for transfers between devices, along_columns(): return lax.ppermute(block, ('section', 'expert'), route)  55.4 us
    ppermute x28, starting transfers between devices, across(): return lax.ppermute(block, ('section', 'expert'), route)  53 us
    pallas_call x14, Pallas kernels, expert_mlp(): pl.pallas_call(mlp_kernel, grid=(hidden // hidden_tile,), in_specs=[pl.Bl...  50.2 us
    unnamed x142, local copies, waits for them, and re-layouts  42.7 us
  transfers between devices with their start and end apart: 127, of which 35 were waited for; matrix products, arithmetic and copies ran while one was open for 3% of the time, Pallas kernels for 4%

profile of v1, /device:TPU:5, one launch (start us, length us, event | category | flops | bytes accessed | tf_op | source)
XLA Modules:
  0.0 766.9 jit_solution(13072094124011492425)
XLA Ops:
  40.0 22.2 %collective-permute-start.27 = (bf16[16,2048]{1,0:T(8,128)(2,1)S(1)}, bf16[16,2048]{1,0:T(8,128)(2,1)S(1)}, u32[]{:S(2)}, u32[]{:S(2)}) collective-permute-start(bf16[16,2048]{1,0:T(8,128)(2,1)S(1)} %get-tuple-element.81), channel_id=1, source_target_pairs={{24,0},{25,1},{26,2},{27,3},{28,4},{29,5},{30,6},{31,7},{0,8},{1,9... | collective-permute-start | bytes 196616 | tf_op jit(solution)/shard_map/ppermute | solution.py:100
  86.2 33.6 %collective-permute-start.45 = (bf16[16,2048]{1,0:T(8,128)(2,1)S(1)}, bf16[16,2048]{1,0:T(8,128)(2,1)S(1)}, u32[]{:S(2)}, u32[]{:S(2)}) collective-permute-start(bf16[16,2048]{1,0:T(8,128)(2,1)S(1)} %get-tuple-element.77), channel_id=1, source_target_pairs={{24,0},{25,1},{26,2},{27,3},{28,4},{29,5},{30,6},{31,7},{0,8},{1,9... | collective-permute-start | bytes 196616 | tf_op jit(solution)/shard_map/ppermute | solution.py:100
  119.7 6.8 collective-permute-start.46
  126.5 6.8 collective-permute-start.47
  133.3 6.8 collective-permute-start.48
  155.0 36.3 %collective-permute-start.63 = (bf16[16,2048]{1,0:T(8,128)(2,1)S(1)}, bf16[16,2048]{1,0:T(8,128)(2,1)S(1)}, u32[]{:S(2)}, u32[]{:S(2)}) collective-permute-start(bf16[16,2048]{1,0:T(8,128)(2,1)S(1)} %get-tuple-element.73), channel_id=1, source_target_pairs={{24,0},{25,1},{26,2},{27,3},{28,4},{29,5},{30,6},{31,7},{0,8},{1,9... | collective-permute-start | bytes 196616 | tf_op jit(solution)/shard_map/ppermute | solution.py:100
  194.0 5.9 collective-permute-start.64
  199.8 5.7 collective-permute-start.65
  205.6 5.7 collective-permute-start.66
  216.1 5.0 collective-permute-start.1
  245.7 5.7 collective-permute-start.70
  251.4 5.7 collective-permute-start.69
  267.2 10.1 %collective-permute-start.82 = (bf16[16,2048]{1,0:T(8,128)(2,1)S(1)}, bf16[16,2048]{1,0:T(8,128)(2,1)S(1)}, u32[]{:S(2)}, u32[]{:S(2)}) collective-permute-start(bf16[16,2048]{1,0:T(8,128)(2,1)S(1)} %get-tuple-element.69), channel_id=1, source_target_pairs={{0,10},{1,11},{2,12},{3,13},{4,14},{5,15},{6,8},{7,9},{8,18},{9,19... | collective-permute-start | bytes 196616 | tf_op jit(solution)/shard_map/ppermute | solution.py:100
  277.3 7.0 collective-permute-start.83
  284.4 7.0 collective-permute-start.84
  298.7 6.0 collective-permute-done.85.other_ref
  316.6 7.9 %collective-permute-start.89 = (bf16[16,2048]{1,0:T(8,128)(2,1)S(1)}, bf16[16,2048]{1,0:T(8,128)(2,1)S(1)}, u32[]{:S(2)}, u32[]{:S(2)}) collective-permute-start(bf16[16,2048]{1,0:T(8,128)(2,1)S(1)} %get-tuple-element.104), channel_id=1, source_target_pairs={{8,10},{9,11},{10,12},{11,13},{12,14},{13,15},{14,8},{15,9},{16,18... | collective-permute-start | bytes 196616 | tf_op jit(solution)/shard_map/ppermute | solution.py:100
  324.5 7.0 collective-permute-start.88
  331.5 7.0 collective-permute-start.87
  350.1 9.0 %collective-permute-start.19 = (bf16[16,2048]{1,0:T(8,128)(2,1)}, bf16[16,2048]{1,0:T(8,128)(2,1)S(1)}, u32[]{:S(2)}, u32[]{:S(2)}) collective-permute-start(bf16[16,2048]{1,0:T(8,128)(2,1)} %get-tuple-element.87), channel_id=1, source_target_pairs={{24,2},{25,3},{26,4},{27,5},{28,6},{29,7},{30,0},{31,1},{0,10},{1,... | collective-permute-start | bytes 196616 | tf_op jit(solution)/shard_map/ppermute | solution.py:100
  397.9 5.2 collective-permute-start.105
  407.0 11.2 %collective-permute-start.36 = (bf16[16,2048]{1,0:T(8,128)(2,1)S(1)}, bf16[16,2048]{1,0:T(8,128)(2,1)S(1)}, u32[]{:S(2)}, u32[]{:S(2)}) collective-permute-start(bf16[16,2048]{1,0:T(8,128)(2,1)S(1)} %get-tuple-element.85), channel_id=1, source_target_pairs={{24,0},{25,1},{26,2},{27,3},{28,4},{29,5},{30,6},{31,7},{0,8},{1,9... | collective-permute-start | bytes 196616 | tf_op jit(solution)/shard_map/ppermute | solution.py:100
  418.1 6.8 collective-permute-start.37
  424.9 6.8 collective-permute-start.38
  431.7 6.8 collective-permute-start.39
  457.3 34.7 %collective-permute-start.54 = (bf16[16,2048]{1,0:T(8,128)(2,1)S(1)}, bf16[16,2048]{1,0:T(8,128)(2,1)S(1)}, u32[]{:S(2)}, u32[]{:S(2)}) collective-permute-start(bf16[16,2048]{1,0:T(8,128)(2,1)S(1)} %get-tuple-element.75), channel_id=1, source_target_pairs={{24,0},{25,1},{26,2},{27,3},{28,4},{29,5},{30,6},{31,7},{0,8},{1,9... | collective-permute-start | bytes 196616 | tf_op jit(solution)/shard_map/ppermute | solution.py:100
  498.0 6.7 collective-permute-start.55
  504.7 5.4 collective-permute-done.55
  512.9 5.9 collective-permute-done.56
  528.5 5.7 collective-permute-done.58.other_ref
  542.4 5.6 collective-permute-done.59
  548.0 6.5 collective-permute-start.62
  554.5 5.7 collective-permute-start.61
  560.3 5.7 collective-permute-start.60
  579.4 5.2 collective-permute-start.73
  584.6 7.0 collective-permute-start.74
  591.7 7.0 collective-permute-start.75
  605.8 6.3 collective-permute-done.76.other_ref
  618.6 5.3 collective-permute-done.77
  624.0 7.9 %collective-permute-start.80 = (bf16[16,2048]{1,0:T(8,128)(2,1)S(1)}, bf16[16,2048]{1,0:T(8,128)(2,1)S(1)}, u32[]{:S(2)}, u32[]{:S(2)}) collective-permute-start(bf16[16,2048]{1,0:T(8,128)(2,1)S(1)} %get-tuple-element.107), channel_id=1, source_target_pairs={{8,10},{9,11},{10,12},{11,13},{12,14},{13,15},{14,8},{15,9},{16,18... | collective-permute-start | bytes 196616 | tf_op jit(solution)/shard_map/ppermute | solution.py:100
  631.9 7.0 collective-permute-start.79
  639.0 7.0 collective-permute-start.78
  646.0 7.0 collective-permute-start.125
  653.0 6.8 collective-permute-start.124
  735.1 7.8 %collective-permute-start.116 = (bf16[16,2048]{1,0:T(8,128)(2,1)S(1)}, bf16[16,2048]{1,0:T(8,128)(2,1)S(1)}, u32[]{:S(2)}, u32[]{:S(2)}) collective-permute-start(bf16[16,2048]{1,0:T(8,128)(2,1)S(1)} %get-tuple-element.95), channel_id=1, source_target_pairs={{24,26},{25,27},{26,28},{27,29},{28,30},{29,31},{30,24},{31,25}} | collective-permute-start | bytes 196616 | tf_op jit(solution)/shard_map/ppermute | solution.py:100
  742.8 6.8 collective-permute-start.115
  749.6 6.8 collective-permute-start.114
  756.4 6.8 collective-permute-start.123
  (443 shorter events, 344.3 us)
Async XLA Ops:
  1.5 14.0 %collective-permute-start.9 = (bf16[16,2048]{1,0:T(8,128)(2,1)S(1)}, bf16[16,2048]{1,0:T(8,128)(2,1)S(1)}, u32[]{:S(2)}, u32[]{:S(2)}) collective-permute-start(bf16[16,2048]{1,0:T(8,128)(2,1)S(1)} %get-tuple-element.89), channel_id=1, source_target_pairs={{24,0},{25,1},{26,2},{27,3},{28,4},{29,5},{30,6},{31,7}} | collective-permute-start | bytes 196616 | tf_op jit(solution)/shard_map/ppermute | solution.py:100
  40.0 30.6 %collective-permute-start.27 = (bf16[16,2048]{1,0:T(8,128)(2,1)S(1)}, bf16[16,2048]{1,0:T(8,128)(2,1)S(1)}, u32[]{:S(2)}, u32[]{:S(2)}) collective-permute-start(bf16[16,2048]{1,0:T(8,128)(2,1)S(1)} %get-tuple-element.81), channel_id=1, source_target_pairs={{24,0},{25,1},{26,2},{27,3},{28,4},{29,5},{30,6},{31,7},{0,8},{1,9... | collective-permute-start | bytes 196616 | tf_op jit(solution)/shard_map/ppermute | solution.py:100
  86.2 53.9 %collective-permute-start.45 = (bf16[16,2048]{1,0:T(8,128)(2,1)S(1)}, bf16[16,2048]{1,0:T(8,128)(2,1)S(1)}, u32[]{:S(2)}, u32[]{:S(2)}) collective-permute-start(bf16[16,2048]{1,0:T(8,128)(2,1)S(1)} %get-tuple-element.77), channel_id=1, source_target_pairs={{24,0},{25,1},{26,2},{27,3},{28,4},{29,5},{30,6},{31,7},{0,8},{1,9... | collective-permute-start | bytes 196616 | tf_op jit(solution)/shard_map/ppermute | solution.py:100
  119.7 20.4 %collective-permute-start.46 = (bf16[16,2048]{1,0:T(8,128)(2,1)S(1)}, bf16[16,2048]{1,0:T(8,128)(2,1)S(1)}, u32[]{:S(2)}, u32[]{:S(2)}) collective-permute-start(bf16[16,2048]{1,0:T(8,128)(2,1)S(1)} %get-tuple-element.77), channel_id=1, source_target_pairs={{24,2},{25,3},{26,4},{27,5},{28,6},{29,7},{30,0},{31,1},{0,10},{1,... | collective-permute-start | bytes 196616 | tf_op jit(solution)/shard_map/ppermute | solution.py:100
  126.5 13.6 %collective-permute-start.47 = (bf16[16,2048]{1,0:T(8,128)(2,1)S(1)}, bf16[16,2048]{1,0:T(8,128)(2,1)S(1)}, u32[]{:S(2)}, u32[]{:S(2)}) collective-permute-start(bf16[16,2048]{1,0:T(8,128)(2,1)S(1)} %get-tuple-element.77), channel_id=1, source_target_pairs={{24,4},{25,5},{26,6},{27,7},{28,0},{29,1},{30,2},{31,3},{0,12},{1,... | collective-permute-start | bytes 196616 | tf_op jit(solution)/shard_map/ppermute | solution.py:100
  155.0 56.3 %collective-permute-start.63 = (bf16[16,2048]{1,0:T(8,128)(2,1)S(1)}, bf16[16,2048]{1,0:T(8,128)(2,1)S(1)}, u32[]{:S(2)}, u32[]{:S(2)}) collective-permute-start(bf16[16,2048]{1,0:T(8,128)(2,1)S(1)} %get-tuple-element.73), channel_id=1, source_target_pairs={{24,0},{25,1},{26,2},{27,3},{28,4},{29,5},{30,6},{31,7},{0,8},{1,9... | collective-permute-start | bytes 196616 | tf_op jit(solution)/shard_map/ppermute | solution.py:100
  191.3 35.5 %collective-permute-start = (bf16[16,2048]{1,0:T(8,128)(2,1)}, bf16[16,2048]{1,0:T(8,128)(2,1)}, u32[]{:S(2)}, u32[]{:S(2)}) collective-permute-start(bf16[16,2048]{1,0:T(8,128)(2,1)} %get-tuple-element.90), channel_id=1, source_target_pairs={{24,0},{25,1},{26,2},{27,3},{28,4},{29,5},{30,6},{31,7}} | collective-permute-start | bytes 196616 | tf_op jit(solution)/shard_map/ppermute | solution.py:100
  194.0 17.3 %collective-permute-start.64 = (bf16[16,2048]{1,0:T(8,128)(2,1)S(1)}, bf16[16,2048]{1,0:T(8,128)(2,1)S(1)}, u32[]{:S(2)}, u32[]{:S(2)}) collective-permute-start(bf16[16,2048]{1,0:T(8,128)(2,1)S(1)} %get-tuple-element.73), channel_id=1, source_target_pairs={{24,2},{25,3},{26,4},{27,5},{28,6},{29,7},{30,0},{31,1},{0,10},{1,... | collective-permute-start | bytes 196616 | tf_op jit(solution)/shard_map/ppermute | solution.py:100
  216.1 20.6 %collective-permute-start.1 = (bf16[16,2048]{1,0:T(8,128)(2,1)}, bf16[16,2048]{1,0:T(8,128)(2,1)}, u32[]{:S(2)}, u32[]{:S(2)}) collective-permute-start(bf16[16,2048]{1,0:T(8,128)(2,1)} %get-tuple-element.90), channel_id=1, source_target_pairs={{24,2},{25,3},{26,4},{27,5},{28,6},{29,7},{30,0},{31,1}} | collective-permute-start | bytes 196616 | tf_op jit(solution)/shard_map/ppermute | solution.py:100
  221.1 16.4 %collective-permute-start.2 = (bf16[16,2048]{1,0:T(8,128)(2,1)}, bf16[16,2048]{1,0:T(8,128)(2,1)}, u32[]{:S(2)}, u32[]{:S(2)}) collective-permute-start(bf16[16,2048]{1,0:T(8,128)(2,1)} %get-tuple-element.90), channel_id=1, source_target_pairs={{24,4},{25,5},{26,6},{27,7},{28,0},{29,1},{30,2},{31,3}} | collective-permute-start | bytes 196616 | tf_op jit(solution)/shard_map/ppermute | solution.py:100
  223.4 33.7 %collective-permute-start.3 = (bf16[16,2048]{1,0:T(8,128)(2,1)}, bf16[16,2048]{1,0:T(8,128)(2,1)}, u32[]{:S(2)}, u32[]{:S(2)}) collective-permute-start(bf16[16,2048]{1,0:T(8,128)(2,1)} %get-tuple-element.90), channel_id=1, source_target_pairs={{24,6},{25,7},{26,0},{27,1},{28,2},{29,3},{30,4},{31,5}} | collective-permute-start | bytes 196616 | tf_op jit(solution)/shard_map/ppermute | solution.py:100
  241.7 16.9 %collective-permute-start.71 = (bf16[16,2048]{1,0:T(8,128)(2,1)S(1)}, bf16[16,2048]{1,0:T(8,128)(2,1)S(1)}, u32[]{:S(2)}, u32[]{:S(2)}) collective-permute-start(bf16[16,2048]{1,0:T(8,128)(2,1)S(1)} %get-tuple-element.110), channel_id=1, source_target_pairs={{0,2},{1,3},{2,4},{3,5},{4,6},{5,7},{6,0},{7,1},{8,10},{9,11},{10,... | collective-permute-start | bytes 196616 | tf_op jit(solution)/shard_map/ppermute | solution.py:100
  262.0 29.4 %collective-permute-start.81 = (bf16[16,2048]{1,0:T(8,128)(2,1)S(1)}, bf16[16,2048]{1,0:T(8,128)(2,1)S(1)}, u32[]{:S(2)}, u32[]{:S(2)}) collective-permute-start(bf16[16,2048]{1,0:T(8,128)(2,1)S(1)} %get-tuple-element.69), channel_id=1, source_target_pairs={{0,8},{1,9},{2,10},{3,11},{4,12},{5,13},{6,14},{7,15},{8,16},{9,17... | collective-permute-start | bytes 196616 | tf_op jit(solution)/shard_map/ppermute | solution.py:100
  266.5 32.1 %collective-permute-start.5 = (bf16[64,2048]{1,0:T(8,128)(2,1)S(1)}, bf16[64,2048]{1,0:T(8,128)(2,1)S(1)}, u32[]{:S(2)}, u32[]{:S(2)}) collective-permute-start(bf16[64,2048]{1,0:T(8,128)(2,1)S(1)} %get-tuple-element.34), channel_id=1, source_target_pairs={{0,1},{1,0},{2,3},{3,2},{4,5},{5,4},{6,7},{7,6}} | collective-permute-start | bytes 786440 | tf_op jit(solution)/shard_map/ppermute | solution.py:104
  267.2 24.2 %collective-permute-start.82 = (bf16[16,2048]{1,0:T(8,128)(2,1)S(1)}, bf16[16,2048]{1,0:T(8,128)(2,1)S(1)}, u32[]{:S(2)}, u32[]{:S(2)}) collective-permute-start(bf16[16,2048]{1,0:T(8,128)(2,1)S(1)} %get-tuple-element.69), channel_id=1, source_target_pairs={{0,10},{1,11},{2,12},{3,13},{4,14},{5,15},{6,8},{7,9},{8,18},{9,19... | collective-permute-start | bytes 196616 | tf_op jit(solution)/shard_map/ppermute | solution.py:100
  277.3 14.1 %collective-permute-start.83 = (bf16[16,2048]{1,0:T(8,128)(2,1)S(1)}, bf16[16,2048]{1,0:T(8,128)(2,1)S(1)}, u32[]{:S(2)}, u32[]{:S(2)}) collective-permute-start(bf16[16,2048]{1,0:T(8,128)(2,1)S(1)} %get-tuple-element.69), channel_id=1, source_target_pairs={{0,12},{1,13},{2,14},{3,15},{4,8},{5,9},{6,10},{7,11},{8,20},{9,21... | collective-permute-start | bytes 196616 | tf_op jit(solution)/shard_map/ppermute | solution.py:100
  311.1 20.4 %collective-permute-start.8 = (bf16[16,2048]{1,0:T(8,128)(2,1)S(1)}, bf16[16,2048]{1,0:T(8,128)(2,1)S(1)}, u32[]{:S(2)}, u32[]{:S(2)}) collective-permute-start(bf16[16,2048]{1,0:T(8,128)(2,1)S(1)} %get-tuple-element.131), channel_id=1, source_target_pairs={{0,2},{1,3},{2,4},{3,5},{4,6},{5,7},{6,0},{7,1}} | collective-permute-start | bytes 196616 | tf_op jit(solution)/shard_map/ppermute | solution.py:100
  311.8 26.8 %collective-permute-start.7 = (bf16[16,2048]{1,0:T(8,128)(2,1)S(1)}, bf16[16,2048]{1,0:T(8,128)(2,1)S(1)}, u32[]{:S(2)}, u32[]{:S(2)}) collective-permute-start(bf16[16,2048]{1,0:T(8,128)(2,1)S(1)} %get-tuple-element.132), channel_id=1, source_target_pairs={{0,4},{1,5},{2,6},{3,7},{4,0},{5,1},{6,2},{7,3}} | collective-permute-start | bytes 196616 | tf_op jit(solution)/shard_map/ppermute | solution.py:100
  312.5 26.1 %collective-permute-start.6 = (bf16[16,2048]{1,0:T(8,128)(2,1)S(1)}, bf16[16,2048]{1,0:T(8,128)(2,1)S(1)}, u32[]{:S(2)}, u32[]{:S(2)}) collective-permute-start(bf16[16,2048]{1,0:T(8,128)(2,1)S(1)} %get-tuple-element.130), channel_id=1, source_target_pairs={{0,6},{1,7},{2,0},{3,1},{4,2},{5,3},{6,4},{7,5}} | collective-permute-start | bytes 196616 | tf_op jit(solution)/shard_map/ppermute | solution.py:100
  316.6 22.0 %collective-permute-start.89 = (bf16[16,2048]{1,0:T(8,128)(2,1)S(1)}, bf16[16,2048]{1,0:T(8,128)(2,1)S(1)}, u32[]{:S(2)}, u32[]{:S(2)}) collective-permute-start(bf16[16,2048]{1,0:T(8,128)(2,1)S(1)} %get-tuple-element.104), channel_id=1, source_target_pairs={{8,10},{9,11},{10,12},{11,13},{12,14},{13,15},{14,8},{15,9},{16,18... | collective-permute-start | bytes 196616 | tf_op jit(solution)/shard_map/ppermute | solution.py:100
  324.5 14.1 %collective-permute-start.88 = (bf16[16,2048]{1,0:T(8,128)(2,1)S(1)}, bf16[16,2048]{1,0:T(8,128)(2,1)S(1)}, u32[]{:S(2)}, u32[]{:S(2)}) collective-permute-start(bf16[16,2048]{1,0:T(8,128)(2,1)S(1)} %get-tuple-element.105), channel_id=1, source_target_pairs={{8,12},{9,13},{10,14},{11,15},{12,8},{13,9},{14,10},{15,11},{16,20... | collective-permute-start | bytes 196616 | tf_op jit(solution)/shard_map/ppermute | solution.py:100
  344.9 14.2 %collective-permute-start.100 = (bf16[16,2048]{1,0:T(8,128)(2,1)S(1)}, bf16[16,2048]{1,0:T(8,128)(2,1)S(1)}, u32[]{:S(2)}, u32[]{:S(2)}) collective-permute-start(bf16[16,2048]{1,0:T(8,128)(2,1)S(1)} %get-tuple-element.65), channel_id=1, source_target_pairs={{8,18},{9,19},{10,20},{11,21},{12,22},{13,23},{14,16},{15,17},{16,... | collective-permute-start | bytes 196616 | tf_op jit(solution)/shard_map/ppermute | solution.py:100
  346.2 15.9 %collective-permute-start.101 = (bf16[16,2048]{1,0:T(8,128)(2,1)S(1)}, bf16[16,2048]{1,0:T(8,128)(2,1)S(1)}, u32[]{:S(2)}, u32[]{:S(2)}) collective-permute-start(bf16[16,2048]{1,0:T(8,128)(2,1)S(1)} %get-tuple-element.65), channel_id=1, source_target_pairs={{8,20},{9,21},{10,22},{11,23},{12,16},{13,17},{14,18},{15,19},{16,... | collective-permute-start | bytes 196616 | tf_op jit(solution)/shard_map/ppermute | solution.py:100
  347.5 18.3 %collective-permute-start.102 = (bf16[16,2048]{1,0:T(8,128)(2,1)S(1)}, bf16[16,2048]{1,0:T(8,128)(2,1)S(1)}, u32[]{:S(2)}, u32[]{:S(2)}) collective-permute-start(bf16[16,2048]{1,0:T(8,128)(2,1)S(1)} %get-tuple-element.65), channel_id=1, source_target_pairs={{8,22},{9,23},{10,16},{11,17},{12,18},{13,19},{14,20},{15,21},{16,... | collective-permute-start | bytes 196616 | tf_op jit(solution)/shard_map/ppermute | solution.py:100
  348.8 20.1 %collective-permute-start.18 = (bf16[16,2048]{1,0:T(8,128)(2,1)}, bf16[16,2048]{1,0:T(8,128)(2,1)S(1)}, u32[]{:S(2)}, u32[]{:S(2)}) collective-permute-start(bf16[16,2048]{1,0:T(8,128)(2,1)} %get-tuple-element.87), channel_id=1, source_target_pairs={{24,0},{25,1},{26,2},{27,3},{28,4},{29,5},{30,6},{31,7},{0,8},{1,9... | collective-permute-start | bytes 196616 | tf_op jit(solution)/shard_map/ppermute | solution.py:100
  350.1 18.8 %collective-permute-start.19 = (bf16[16,2048]{1,0:T(8,128)(2,1)}, bf16[16,2048]{1,0:T(8,128)(2,1)S(1)}, u32[]{:S(2)}, u32[]{:S(2)}) collective-permute-start(bf16[16,2048]{1,0:T(8,128)(2,1)} %get-tuple-element.87), channel_id=1, source_target_pairs={{24,2},{25,3},{26,4},{27,5},{28,6},{29,7},{30,0},{31,1},{0,10},{1,... | collective-permute-start | bytes 196616 | tf_op jit(solution)/shard_map/ppermute | solution.py:100
  369.1 15.5 %collective-permute-start.22 = (bf16[64,2048]{1,0:T(8,128)(2,1)S(1)}, bf16[64,2048]{1,0:T(8,128)(2,1)}, u32[]{:S(2)}, u32[]{:S(2)}) collective-permute-start(bf16[64,2048]{1,0:T(8,128)(2,1)S(1)} %constant_dynamic-update-slice_fusion.8.own_ref), channel_id=1, source_target_pairs={{0,1},{1,0},{2,3},{3,2},{4,5},{5,4},{6,7},{7,6},{8,9},{9,8},{10,11... | collective-permute-start | bytes 786440 | tf_op jit(solution)/shard_map/ppermute | solution.py:104
  407.0 31.5 %collective-permute-start.36 = (bf16[16,2048]{1,0:T(8,128)(2,1)S(1)}, bf16[16,2048]{1,0:T(8,128)(2,1)S(1)}, u32[]{:S(2)}, u32[]{:S(2)}) collective-permute-start(bf16[16,2048]{1,0:T(8,128)(2,1)S(1)} %get-tuple-element.85), channel_id=1, source_target_pairs={{24,0},{25,1},{26,2},{27,3},{28,4},{29,5},{30,6},{31,7},{0,8},{1,9... | collective-permute-start | bytes 196616 | tf_op jit(solution)/shard_map/ppermute | solution.py:100
  418.1 20.3 %collective-permute-start.37 = (bf16[16,2048]{1,0:T(8,128)(2,1)S(1)}, bf16[16,2048]{1,0:T(8,128)(2,1)S(1)}, u32[]{:S(2)}, u32[]{:S(2)}) collective-permute-start(bf16[16,2048]{1,0:T(8,128)(2,1)S(1)} %get-tuple-element.85), channel_id=1, source_target_pairs={{24,2},{25,3},{26,4},{27,5},{28,6},{29,7},{30,0},{31,1},{0,10},{1,... | collective-permute-start | bytes 196616 | tf_op jit(solution)/shard_map/ppermute | solution.py:100
  424.9 13.6 %collective-permute-start.38 = (bf16[16,2048]{1,0:T(8,128)(2,1)S(1)}, bf16[16,2048]{1,0:T(8,128)(2,1)S(1)}, u32[]{:S(2)}, u32[]{:S(2)}) collective-permute-start(bf16[16,2048]{1,0:T(8,128)(2,1)S(1)} %get-tuple-element.85), channel_id=1, source_target_pairs={{24,4},{25,5},{26,6},{27,7},{28,0},{29,1},{30,2},{31,3},{0,12},{1,... | collective-permute-start | bytes 196616 | tf_op jit(solution)/shard_map/ppermute | solution.py:100
  457.3 40.7 %collective-permute-start.54 = (bf16[16,2048]{1,0:T(8,128)(2,1)S(1)}, bf16[16,2048]{1,0:T(8,128)(2,1)S(1)}, u32[]{:S(2)}, u32[]{:S(2)}) collective-permute-start(bf16[16,2048]{1,0:T(8,128)(2,1)S(1)} %get-tuple-element.75), channel_id=1, source_target_pairs={{24,0},{25,1},{26,2},{27,3},{28,4},{29,5},{30,6},{31,7},{0,8},{1,9... | collective-permute-start | bytes 196616 | tf_op jit(solution)/shard_map/ppermute | solution.py:100
  492.8 35.7 %collective-permute-start.117 = (bf16[16,2048]{1,0:T(8,128)(2,1)}, bf16[16,2048]{1,0:T(8,128)(2,1)S(1)}, u32[]{:S(2)}, u32[]{:S(2)}) collective-permute-start(bf16[16,2048]{1,0:T(8,128)(2,1)} %get-tuple-element.61), channel_id=1, source_target_pairs={{16,24},{17,25},{18,26},{19,27},{20,28},{21,29},{22,30},{23,31}} | collective-permute-start | bytes 196616 | tf_op jit(solution)/shard_map/ppermute | solution.py:100
  494.1 48.3 %collective-permute-start.118 = (bf16[16,2048]{1,0:T(8,128)(2,1)}, bf16[16,2048]{1,0:T(8,128)(2,1)S(1)}, u32[]{:S(2)}, u32[]{:S(2)}) collective-permute-start(bf16[16,2048]{1,0:T(8,128)(2,1)} %get-tuple-element.61), channel_id=1, source_target_pairs={{16,26},{17,27},{18,28},{19,29},{20,30},{21,31},{22,24},{23,25}} | collective-permute-start | bytes 196616 | tf_op jit(solution)/shard_map/ppermute | solution.py:100
  495.4 47.0 %collective-permute-start.119 = (bf16[16,2048]{1,0:T(8,128)(2,1)}, bf16[16,2048]{1,0:T(8,128)(2,1)S(1)}, u32[]{:S(2)}, u32[]{:S(2)}) collective-permute-start(bf16[16,2048]{1,0:T(8,128)(2,1)} %get-tuple-element.61), channel_id=1, source_target_pairs={{16,28},{17,29},{18,30},{19,31},{20,24},{21,25},{22,26},{23,27}} | collective-permute-start | bytes 196616 | tf_op jit(solution)/shard_map/ppermute | solution.py:100
  496.7 69.3 %collective-permute-start.120 = (bf16[16,2048]{1,0:T(8,128)(2,1)}, bf16[16,2048]{1,0:T(8,128)(2,1)S(1)}, u32[]{:S(2)}, u32[]{:S(2)}) collective-permute-start(bf16[16,2048]{1,0:T(8,128)(2,1)} %get-tuple-element.61), channel_id=1, source_target_pairs={{16,30},{17,31},{18,24},{19,25},{20,26},{21,27},{22,28},{23,29}} | collective-permute-start | bytes 196616 | tf_op jit(solution)/shard_map/ppermute | solution.py:100
  548.0 21.1 %collective-permute-start.62 = (bf16[16,2048]{1,0:T(8,128)(2,1)S(1)}, bf16[16,2048]{1,0:T(8,128)(2,1)S(1)}, u32[]{:S(2)}, u32[]{:S(2)}) collective-permute-start(bf16[16,2048]{1,0:T(8,128)(2,1)S(1)} %get-tuple-element.113), channel_id=1, source_target_pairs={{0,2},{1,3},{2,4},{3,5},{4,6},{5,7},{6,0},{7,1},{8,10},{9,11},{10,... | collective-permute-start | bytes 196616 | tf_op jit(solution)/shard_map/ppermute | solution.py:100
  554.5 14.6 %collective-permute-start.61 = (bf16[16,2048]{1,0:T(8,128)(2,1)S(1)}, bf16[16,2048]{1,0:T(8,128)(2,1)S(1)}, u32[]{:S(2)}, u32[]{:S(2)}) collective-permute-start(bf16[16,2048]{1,0:T(8,128)(2,1)S(1)} %get-tuple-element.114), channel_id=1, source_target_pairs={{0,4},{1,5},{2,6},{3,7},{4,0},{5,1},{6,2},{7,3},{8,12},{9,13},{10,... | collective-permute-start | bytes 196616 | tf_op jit(solution)/shard_map/ppermute | solution.py:100
  570.3 28.4 %collective-permute-start.72 = (bf16[16,2048]{1,0:T(8,128)(2,1)S(1)}, bf16[16,2048]{1,0:T(8,128)(2,1)S(1)}, u32[]{:S(2)}, u32[]{:S(2)}) collective-permute-start(bf16[16,2048]{1,0:T(8,128)(2,1)S(1)} %get-tuple-element.71), channel_id=1, source_target_pairs={{0,8},{1,9},{2,10},{3,11},{4,12},{5,13},{6,14},{7,15},{8,16},{9,17... | collective-permute-start | bytes 196616 | tf_op jit(solution)/shard_map/ppermute | solution.py:100
  576.3 42.2 %collective-permute-start.122 = (bf16[64,2048]{1,0:T(8,128)(2,1)S(1)}, bf16[64,2048]{1,0:T(8,128)(2,1)S(1)}, u32[]{:S(2)}, u32[]{:S(2)}) collective-permute-start(bf16[64,2048]{1,0:T(8,128)(2,1)S(1)} %get-tuple-element.60), channel_id=1, source_target_pairs={{24,25},{25,24},{26,27},{27,26},{28,29},{29,28},{30,31},{31,30}} | collective-permute-start | bytes 786440 | tf_op jit(solution)/shard_map/ppermute | solution.py:104
  579.4 19.3 %collective-permute-start.73 = (bf16[16,2048]{1,0:T(8,128)(2,1)S(1)}, bf16[16,2048]{1,0:T(8,128)(2,1)S(1)}, u32[]{:S(2)}, u32[]{:S(2)}) collective-permute-start(bf16[16,2048]{1,0:T(8,128)(2,1)S(1)} %get-tuple-element.71), channel_id=1, source_target_pairs={{0,10},{1,11},{2,12},{3,13},{4,14},{5,15},{6,8},{7,9},{8,18},{9,19... | collective-permute-start | bytes 196616 | tf_op jit(solution)/shard_map/ppermute | solution.py:100
  584.6 14.1 %collective-permute-start.74 = (bf16[16,2048]{1,0:T(8,128)(2,1)S(1)}, bf16[16,2048]{1,0:T(8,128)(2,1)S(1)}, u32[]{:S(2)}, u32[]{:S(2)}) collective-permute-start(bf16[16,2048]{1,0:T(8,128)(2,1)S(1)} %get-tuple-element.71), channel_id=1, source_target_pairs={{0,12},{1,13},{2,14},{3,15},{4,8},{5,9},{6,10},{7,11},{8,20},{9,21... | collective-permute-start | bytes 196616 | tf_op jit(solution)/shard_map/ppermute | solution.py:100
  624.0 35.8 %collective-permute-start.80 = (bf16[16,2048]{1,0:T(8,128)(2,1)S(1)}, bf16[16,2048]{1,0:T(8,128)(2,1)S(1)}, u32[]{:S(2)}, u32[]{:S(2)}) collective-permute-start(bf16[16,2048]{1,0:T(8,128)(2,1)S(1)} %get-tuple-element.107), channel_id=1, source_target_pairs={{8,10},{9,11},{10,12},{11,13},{12,14},{13,15},{14,8},{15,9},{16,18... | collective-permute-start | bytes 196616 | tf_op jit(solution)/shard_map/ppermute | solution.py:100
  631.9 27.9 %collective-permute-start.79 = (bf16[16,2048]{1,0:T(8,128)(2,1)S(1)}, bf16[16,2048]{1,0:T(8,128)(2,1)S(1)}, u32[]{:S(2)}, u32[]{:S(2)}) collective-permute-start(bf16[16,2048]{1,0:T(8,128)(2,1)S(1)} %get-tuple-element.108), channel_id=1, source_target_pairs={{8,12},{9,13},{10,14},{11,15},{12,8},{13,9},{14,10},{15,11},{16,20... | collective-permute-start | bytes 196616 | tf_op jit(solution)/shard_map/ppermute | solution.py:100
  639.0 20.9 %collective-permute-start.78 = (bf16[16,2048]{1,0:T(8,128)(2,1)S(1)}, bf16[16,2048]{1,0:T(8,128)(2,1)S(1)}, u32[]{:S(2)}, u32[]{:S(2)}) collective-permute-start(bf16[16,2048]{1,0:T(8,128)(2,1)S(1)} %get-tuple-element.106), channel_id=1, source_target_pairs={{8,14},{9,15},{10,8},{11,9},{12,10},{13,11},{14,12},{15,13},{16,22... | collective-permute-start | bytes 196616 | tf_op jit(solution)/shard_map/ppermute | solution.py:100
  646.0 117.3 %collective-permute-start.125 = (bf16[16,2048]{1,0:T(8,128)(2,1)S(1)}, bf16[16,2048]{1,0:T(8,128)(2,1)S(1)}, u32[]{:S(2)}, u32[]{:S(2)}) collective-permute-start(bf16[16,2048]{1,0:T(8,128)(2,1)S(1)} %get-tuple-element.92), channel_id=1, source_target_pairs={{24,26},{25,27},{26,28},{27,29},{28,30},{29,31},{30,24},{31,25}} | collective-permute-start | bytes 196616 | tf_op jit(solution)/shard_map/ppermute | solution.py:100
  653.0 110.2 %collective-permute-start.124 = (bf16[16,2048]{1,0:T(8,128)(2,1)S(1)}, bf16[16,2048]{1,0:T(8,128)(2,1)S(1)}, u32[]{:S(2)}, u32[]{:S(2)}) collective-permute-start(bf16[16,2048]{1,0:T(8,128)(2,1)S(1)} %get-tuple-element.93), channel_id=1, source_target_pairs={{24,28},{25,29},{26,30},{27,31},{28,24},{29,25},{30,26},{31,27}} | collective-permute-start | bytes 196616 | tf_op jit(solution)/shard_map/ppermute | solution.py:100
  735.1 21.3 %collective-permute-start.116 = (bf16[16,2048]{1,0:T(8,128)(2,1)S(1)}, bf16[16,2048]{1,0:T(8,128)(2,1)S(1)}, u32[]{:S(2)}, u32[]{:S(2)}) collective-permute-start(bf16[16,2048]{1,0:T(8,128)(2,1)S(1)} %get-tuple-element.95), channel_id=1, source_target_pairs={{24,26},{25,27},{26,28},{27,29},{28,30},{29,31},{30,24},{31,25}} | collective-permute-start | bytes 196616 | tf_op jit(solution)/shard_map/ppermute | solution.py:100
  742.8 20.4 %collective-permute-start.115 = (bf16[16,2048]{1,0:T(8,128)(2,1)S(1)}, bf16[16,2048]{1,0:T(8,128)(2,1)S(1)}, u32[]{:S(2)}, u32[]{:S(2)}) collective-permute-start(bf16[16,2048]{1,0:T(8,128)(2,1)S(1)} %get-tuple-element.96), channel_id=1, source_target_pairs={{24,28},{25,29},{26,30},{27,31},{28,24},{29,25},{30,26},{31,27}} | collective-permute-start | bytes 196616 | tf_op jit(solution)/shard_map/ppermute | solution.py:100
  (122 other events, 965.9 us)

commit v2 on v1

v2 whole, which is shorter than its diff:
```python
import functools

import jax
import jax.numpy as jnp
from jax import lax
from jax.experimental import pallas as pl
from jax.experimental.pallas import tpu as pltpu
from jax.sharding import PartitionSpec as P

epsilon = 1e-06
hidden_tile = 256
unrolled_experts = 8


def mlp_kernel(
    own_ref, other_ref, weight_ref, gate_hbm, up_hbm, down_hbm, keep_ref, give_ref,
    gate_ref, up_ref, down_ref, normed_ref, total_ref, arrived,
):
    half = own_ref.shape[0]
    tiles = gate_hbm.shape[1] // hidden_tile
    copies = []
    for tile in range(tiles):
        place = pl.ds(tile * hidden_tile, hidden_tile)
        copies.append(
            (
                pltpu.make_async_copy(gate_hbm.at[:, place], gate_ref.at[tile], arrived.at[tile, 0]),
                pltpu.make_async_copy(up_hbm.at[:, place], up_ref.at[tile], arrived.at[tile, 1]),
                pltpu.make_async_copy(down_hbm.at[place, :], down_ref.at[tile], arrived.at[tile, 2]),
            )
        )
    for group in copies:
        for copy in group:
            copy.start()
    for side, rows_ref in enumerate((own_ref, other_ref)):
        widened = rows_ref[...].astype(jnp.float32)
        inverse_rms = lax.rsqrt(jnp.mean(widened * widened, axis=-1, keepdims=True) + epsilon)
        normed_ref[side * half : (side + 1) * half, :] = (widened * inverse_rms).astype(jnp.bfloat16)
    normed = normed_ref[...]
    for tile in range(tiles):
        copies[tile][0].wait()
        gate_part = jnp.dot(normed, gate_ref[tile], preferred_element_type=jnp.float32)
        copies[tile][1].wait()
        up_part = jnp.dot(normed, up_ref[tile], preferred_element_type=jnp.float32)
        activated = (gate_part / (1.0 + jnp.exp(-gate_part)) * up_part).astype(jnp.bfloat16)
        copies[tile][2].wait()
        partial = jnp.dot(activated, down_ref[tile], preferred_element_type=jnp.float32)
        if tile == 0:
            total_ref[...] = partial
        else:
            total_ref[...] += partial
    weighted = total_ref[...] * weight_ref[...]
    keep_ref[...] = weighted[:half].astype(jnp.bfloat16)
    give_ref[...] = weighted[half:].astype(jnp.bfloat16)


def expert_mlp(own, other, weights, gate_matrix, up_matrix, down_matrix):
    half, features = own.shape
    rows = 2 * half
    hidden = gate_matrix.shape[1]
    tiles = hidden // hidden_tile
    in_vmem = pl.BlockSpec(memory_space=pltpu.VMEM)
    in_hbm = pl.BlockSpec(memory_space=pltpu.HBM)
    return pl.pallas_call(
        mlp_kernel,
        in_specs=[in_vmem] * 3 + [in_hbm] * 3,
        out_specs=[in_vmem] * 2,
        out_shape=[jax.ShapeDtypeStruct((half, features), jnp.bfloat16)] * 2,
        scratch_shapes=[
            pltpu.VMEM((tiles, features, hidden_tile), jnp.bfloat16),
            pltpu.VMEM((tiles, features, hidden_tile), jnp.bfloat16),
            pltpu.VMEM((tiles, hidden_tile, features), jnp.bfloat16),
            pltpu.VMEM((rows, features), jnp.bfloat16),
            pltpu.VMEM((rows, features), jnp.float32),
            pltpu.SemaphoreType.DMA((tiles, 3)),
        ],
        compiler_params=pltpu.CompilerParams(vmem_limit_bytes=40 * 1024 * 1024),
        cost_estimate=pl.CostEstimate(
            flops=6 * rows * features * hidden, bytes_accessed=6 * features * hidden, transcendentals=rows * hidden
        ),
        name="expert_mlp",
    )(own, other, weights, gate_matrix, up_matrix, down_matrix)


def body(tokens_in, expert_ids, gate_values, expert_gate, expert_up, expert_down):
    sections = lax.axis_size("section")
    section_now = lax.axis_index("section")
    experts = lax.axis_size("expert")
    my_expert = lax.axis_index("expert")
    columns = experts // 2
    my_column, my_side = my_expert // 2, my_expert % 2
    batches, row_count, features = tokens_in.shape
    gate_matrix, up_matrix, down_matrix = expert_gate[0, 0], expert_up[0, 0], expert_down[0, 0]
    half = columns * row_count

    my_routes = lax.dynamic_slice_in_dim(expert_ids[0], my_expert * row_count, row_count, 1)
    named = my_routes[None] == jnp.arange(experts, dtype=jnp.int32)[:, None, None, None]
    token_weights = jnp.sum(jnp.where(named, gate_values[0][None], 0.0), axis=3)
    token_weights = lax.all_to_all(token_weights, "expert", split_axis=0, concat_axis=0, tiled=True)
    apart = jnp.arange(columns, dtype=jnp.int32)
    sources = (my_column - apart) % columns * 2
    order = jnp.concatenate([sources + my_side, sources + 1 - my_side])
    token_weights = token_weights[order].transpose(1, 0, 2).reshape(batches, 2 * half, 1)

    def along_columns(block, apart, source_step):
        route = []
        for section in range(sections):
            for column in range(columns):
                for side in range(2):
                    source = (section - source_step) % sections * experts + column * 2 + side
                    route.append((source, section * experts + (column + apart) % columns * 2 + side))
        return lax.ppermute(block, ("section", "expert"), route)

    def across(block):
        return lax.ppermute(block, "expert", [(e, e ^ 1) for e in range(experts)])

    def added(*terms):
        return functools.reduce(jnp.add, [term.astype(jnp.float32) for term in terms])

    def one_slot(slot, state, opening=True, closing=True):
        result, residual, keep, give = state
        if opening:
            fresh = lax.dynamic_index_in_dim(tokens_in, jnp.minimum(slot, batches - 1), 0, keepdims=False)
            payload = fresh if result is None else jnp.where(section_now == sections - 1, fresh, result)
            gathered = [along_columns(payload, d, 1) for d in range(columns)]
        if closing:
            received = across(give)
            summed = added(keep, received).astype(jnp.bfloat16).reshape(columns, row_count, features)
            returned = [along_columns(summed[d], -d, 0) for d in range(1, columns)]
            result = added(residual, summed[0], *returned).astype(jnp.bfloat16)
        if opening:
            own = jnp.concatenate(gathered, axis=0)
            other = across(own)
            round_now = jnp.clip(slot - 2 * section_now, 0, batches - 1)
            weights = lax.dynamic_index_in_dim(token_weights, round_now, 0, keepdims=False)
            residual = gathered[0]
            keep, give = expert_mlp(own, other, weights, gate_matrix, up_matrix, down_matrix)
        return (result, residual, keep, give)

    slots = 2 * sections + batches - 1
    state = (None, None, None, None)
    if experts <= unrolled_experts:
        results = []
        for slot in range(slots):
            state = one_slot(slot, state, slot < slots - 1, slot > 0)
            results.append(state[0])
        results = jnp.stack(results[1:])
    else:
        blank = jnp.zeros((half, features), jnp.bfloat16)
        rows_blank = jnp.zeros((row_count, features), jnp.bfloat16)

        def looped(slot, carried):
            state = one_slot(slot, carried[0])
            return state, lax.dynamic_update_index_in_dim(carried[1], state[0], slot, 0)

        kept = jnp.zeros((slots, row_count, features), jnp.bfloat16)
        results = lax.fori_loop(0, slots, looped, ((rows_blank, rows_blank, blank, blank), kept))[1][1:]
    return lax.dynamic_slice_in_dim(results, 2 * section_now, batches, 0)[None]


def solution(mesh):
    return jax.shard_map(
        body,
        mesh=mesh,
        in_specs=(
            P(None, "expert", None),
            P("section", None, None, None),
            P("section", None, "expert", None),
            P("section", "expert", None, None),
            P("section", "expert", None, None),
            P("section", "expert", None, None),
        ),
        out_specs=P("section", None, "expert", None),
        check_vma=False,
    )
```

time: 771 us -> 535 us (0.69)
  the two profiles are of different devices: /device:TPU:5 before, /device:TPU:0 now
where the time goes in v2:
time: 535 us; the launch traced here: 525 us
  waiting for transfers between devices  225 us (42%)
  starting transfers between devices  165 us (31%)
  Pallas kernels  64 us (12%)
  local copies, waits for them, and re-layouts  52 us (10%)
  other arithmetic  17.7 us (3%)
    ppermute x98, starting transfers between devices, along_columns(): return lax.ppermute(block, ('section', 'expert'), route)  127 us
    ppermute x28, waiting for transfers between devices, across(): return lax.ppermute(block, 'expert', [(e, e ^ 1) for e in range(experts)])  118 us
    ppermute x98, waiting for transfers between devices, along_columns(): return lax.ppermute(block, ('section', 'expert'), route)  104 us
    pallas_call x14, Pallas kernels, expert_mlp(): pl.pallas_call(mlp_kernel, in_specs=[in_vmem] * 3 + [in_hbm] * 3, out_spe...  64 us
    unnamed x142, local copies, waits for them, and re-layouts  42.7 us
    ppermute x28, starting transfers between devices, across(): return lax.ppermute(block, 'expert', [(e, e ^ 1) for e in range(experts)])  35.2 us
    select_n x10, other arithmetic, one_slot(): jnp.where(section_now == sections - 1, fresh, result)  13.1 us
  transfers between devices with their start and end apart: 127, of which 77 were waited for; matrix products, arithmetic and copies ran while one was open for 4% of the time, Pallas kernels for 8%

profile of v2, /device:TPU:0, one launch (start us, length us, event | category | flops | bytes accessed | tf_op | source)
XLA Modules:
  0.0 525.2 jit_solution(13048687246258734646)
XLA Ops:
  2.0 3.8 collective-permute-start.10
  11.0 3.3 all-to-all-start
  17.0 3.7 all-to-all-done
  30.5 4.1 expert_mlp.15
  36.2 5.6 %collective-permute-done.14 = bf16[64,2048]{1,0:T(8,128)(2,1)S(1)} collective-permute-done((bf16[64,2048]{1,0:T(8,128)(2,1)S(1)}, bf16[64,2048]{1,0:T(8,128)(2,1)S(1)}, u32[]{:S(2)}, u32[]{:S(2)}) %collective-permute-start.14) | collective-permute-done | bytes 262176 | tf_op jit(solution)/shard_map/ppermute | solution.py:114
  58.8 3.8 collective-permute-done.29
  65.2 6.1 %collective-permute-done.31.other_ref = bf16[64,2048]{1,0:T(8,128)(2,1)} collective-permute-done((bf16[64,2048]{1,0:T(8,128)(2,1)S(1)}, bf16[64,2048]{1,0:T(8,128)(2,1)}, u32[]{:S(2)}, u32[]{:S(2)}) %collective-permute-start.31) | collective-permute-done | bytes 262176 | tf_op jit(solution)/shard_map/ppermute | solution.py:114
  75.1 5.1 expert_mlp.17
  81.7 5.9 %collective-permute-done.32 = bf16[64,2048]{1,0:T(8,128)(2,1)S(1)} collective-permute-done((bf16[64,2048]{1,0:T(8,128)(2,1)S(1)}, bf16[64,2048]{1,0:T(8,128)(2,1)S(1)}, u32[]{:S(2)}, u32[]{:S(2)}) %collective-permute-start.32) | collective-permute-done | bytes 262176 | tf_op jit(solution)/shard_map/ppermute | solution.py:114
  103.9 3.5 collective-permute-done.47
  109.0 6.1 %collective-permute-done.49.other_ref = bf16[64,2048]{1,0:T(8,128)(2,1)} collective-permute-done((bf16[64,2048]{1,0:T(8,128)(2,1)S(1)}, bf16[64,2048]{1,0:T(8,128)(2,1)}, u32[]{:S(2)}, u32[]{:S(2)}) %collective-permute-start.49) | collective-permute-done | bytes 262176 | tf_op jit(solution)/shard_map/ppermute | solution.py:114
  118.9 5.1 expert_mlp.19
  125.5 5.2 collective-permute-done.50
  146.2 4.0 collective-permute-done.64
  164.3 5.1 expert_mlp.21
  172.4 6.2 %collective-permute-done.68 = bf16[64,2048]{1,0:T(8,128)(2,1)S(1)} collective-permute-done((bf16[64,2048]{1,0:T(8,128)(2,1)S(1)}, bf16[64,2048]{1,0:T(8,128)(2,1)S(1)}, u32[]{:S(2)}, u32[]{:S(2)}) %collective-permute-start.68) | collective-permute-done | bytes 262176 | tf_op jit(solution)/shard_map/ppermute | solution.py:114
  191.3 4.1 expert_mlp.14
  199.8 3.2 collective-permute-done.82
  205.3 7.0 %collective-permute-done.85.other_ref = bf16[64,2048]{1,0:T(8,128)(2,1)S(1)} collective-permute-done((bf16[64,2048]{1,0:T(8,128)(2,1)S(1)}, bf16[64,2048]{1,0:T(8,128)(2,1)S(1)}, u32[]{:S(2)}, u32[]{:S(2)}) %collective-permute-start.85) | collective-permute-done | bytes 262176 | tf_op jit(solution)/shard_map/ppermute | solution.py:114
  212.3 4.1 expert_mlp.23
  259.0 4.8 expert_mlp.25
  270.3 5.1 expert_mlp.16
  276.7 3.2 collective-permute-start.107
  284.9 3.4 collective-permute-start.24
  300.8 3.7 collective-permute-done.38
  305.4 7.4 %collective-permute-done.40.other_ref = bf16[64,2048]{1,0:T(8,128)(2,1)} collective-permute-done((bf16[64,2048]{1,0:T(8,128)(2,1)S(1)}, bf16[64,2048]{1,0:T(8,128)(2,1)}, u32[]{:S(2)}, u32[]{:S(2)}) %collective-permute-start.40) | collective-permute-done | bytes 262176 | tf_op jit(solution)/shard_map/ppermute | solution.py:114
  316.6 5.8 %expert_mlp.18 = (bf16[64,2048]{1,0:T(8,128)(2,1)S(1)}, bf16[64,2048]{1,0:T(8,128)(2,1)}) custom-call(bf16[64,2048]{1,0:T(8,128)(2,1)S(1)} %constant_dynamic-update-slice_fusion.16.own_ref, bf16[64,2048]{1,0:T(8,128)(2,1)} %collective-permute-done.40.other_ref, f32[128,1]{1,0:T(8,128)S(1)} %copy.60.weight_ref, bf16[2048,768]{1,0:T(8,128)(2,1)S(1)} %bitcast.105, ...), custom_call_target="tpu_custom_call" | custom-call | flops 1207959552 | bytes 9437184 | tf_op jit(solution)/shard_map/expert_mlp/pallas_call | solution.py:63
  324.3 6.3 %collective-permute-done.41 = bf16[64,2048]{1,0:T(8,128)(2,1)} collective-permute-done((bf16[64,2048]{1,0:T(8,128)(2,1)}, bf16[64,2048]{1,0:T(8,128)(2,1)}, u32[]{:S(2)}, u32[]{:S(2)}) %collective-permute-start.41) | collective-permute-done | bytes 262176 | tf_op jit(solution)/shard_map/ppermute | solution.py:114
  347.8 6.1 %collective-permute-done.55 = bf16[16,2048]{1,0:T(8,128)(2,1)S(1)} collective-permute-done((bf16[16,2048]{1,0:T(8,128)(2,1)S(1)}, bf16[16,2048]{1,0:T(8,128)(2,1)S(1)}, u32[]{:S(2)}, u32[]{:S(2)}) %collective-permute-start.55) | collective-permute-done | bytes 65568 | tf_op jit(solution)/shard_map/ppermute | solution.py:111
  355.0 5.0 collective-permute-done.56
  360.2 4.6 collective-permute-done.57
  366.7 5.7 %collective-permute-done.58.other_ref = bf16[64,2048]{1,0:T(8,128)(2,1)S(1)} collective-permute-done((bf16[64,2048]{1,0:T(8,128)(2,1)S(1)}, bf16[64,2048]{1,0:T(8,128)(2,1)S(1)}, u32[]{:S(2)}, u32[]{:S(2)}) %collective-permute-start.58) | collective-permute-done | bytes 262176 | tf_op jit(solution)/shard_map/ppermute | solution.py:114
  376.2 4.1 expert_mlp.20
  381.9 5.4 %collective-permute-done.59 = bf16[64,2048]{1,0:T(8,128)(2,1)S(1)} collective-permute-done((bf16[64,2048]{1,0:T(8,128)(2,1)S(1)}, bf16[64,2048]{1,0:T(8,128)(2,1)S(1)}, u32[]{:S(2)}, u32[]{:S(2)}) %collective-permute-start.59) | collective-permute-done | bytes 262176 | tf_op jit(solution)/shard_map/ppermute | solution.py:114
  396.5 3.5 collective-permute-done.121.other_ref
  399.9 4.1 expert_mlp.27
  408.1 3.4 collective-permute-done.73
  414.5 5.8 %collective-permute-done.76.other_ref = bf16[64,2048]{1,0:T(8,128)(2,1)S(1)} collective-permute-done((bf16[64,2048]{1,0:T(8,128)(2,1)S(1)}, bf16[64,2048]{1,0:T(8,128)(2,1)S(1)}, u32[]{:S(2)}, u32[]{:S(2)}) %collective-permute-start.76) | collective-permute-done | bytes 262176 | tf_op jit(solution)/shard_map/ppermute | solution.py:114
  420.3 4.1 expert_mlp.22
  425.6 5.8 %collective-permute-done.77 = bf16[64,2048]{1,0:T(8,128)(2,1)S(1)} collective-permute-done((bf16[64,2048]{1,0:T(8,128)(2,1)S(1)}, bf16[64,2048]{1,0:T(8,128)(2,1)S(1)}, u32[]{:S(2)}, u32[]{:S(2)}) %collective-permute-start.77) | collective-permute-done | bytes 262176 | tf_op jit(solution)/shard_map/ppermute | solution.py:114
  438.2 3.6 collective-permute-done.79
  442.8 4.6 collective-permute-start.91
  455.5 7.1 %collective-permute-done.94.other_ref = bf16[64,2048]{1,0:T(8,128)(2,1)S(1)} collective-permute-done((bf16[64,2048]{1,0:T(8,128)(2,1)S(1)}, bf16[64,2048]{1,0:T(8,128)(2,1)S(1)}, u32[]{:S(2)}, u32[]{:S(2)}) %collective-permute-start.94) | collective-permute-done | bytes 262176 | tf_op jit(solution)/shard_map/ppermute | solution.py:114
  462.7 4.1 expert_mlp.24
  468.1 6.3 %collective-permute-done.95 = bf16[64,2048]{1,0:T(8,128)(2,1)S(1)} collective-permute-done((bf16[64,2048]{1,0:T(8,128)(2,1)S(1)}, bf16[64,2048]{1,0:T(8,128)(2,1)S(1)}, u32[]{:S(2)}, u32[]{:S(2)}) %collective-permute-start.95) | collective-permute-done | bytes 262176 | tf_op jit(solution)/shard_map/ppermute | solution.py:114
  494.2 6.9 %collective-permute-done.112.other_ref = bf16[64,2048]{1,0:T(8,128)(2,1)S(1)} collective-permute-done((bf16[64,2048]{1,0:T(8,128)(2,1)S(1)}, bf16[64,2048]{1,0:T(8,128)(2,1)S(1)}, u32[]{:S(2)}, u32[]{:S(2)}) %collective-permute-start.112) | collective-permute-done | bytes 262176 | tf_op jit(solution)/shard_map/ppermute | solution.py:114
  501.1 4.1 expert_mlp.26
  506.5 6.2 %collective-permute-done.113 = bf16[64,2048]{1,0:T(8,128)(2,1)S(1)} collective-permute-done((bf16[64,2048]{1,0:T(8,128)(2,1)S(1)}, bf16[64,2048]{1,0:T(8,128)(2,1)S(1)}, u32[]{:S(2)}, u32[]{:S(2)}) %collective-permute-start.113) | collective-permute-done | bytes 262176 | tf_op jit(solution)/shard_map/ppermute | solution.py:114
  (443 shorter events, 288.6 us)
Async XLA Ops:
  1.5 12.8 %collective-permute-start.9 = (bf16[16,2048]{1,0:T(8,128)(2,1)S(1)}, bf16[16,2048]{1,0:T(8,128)(2,1)S(1)}, u32[]{:S(2)}, u32[]{:S(2)}) collective-permute-start(bf16[16,2048]{1,0:T(8,128)(2,1)S(1)} %get-tuple-element.89), channel_id=1, source_target_pairs={{24,0},{25,1},{26,2},{27,3},{28,4},{29,5},{30,6},{31,7},{0,8},{1,9... | collective-permute-start | bytes 196616 | tf_op jit(solution)/shard_map/ppermute | solution.py:111
  2.0 12.4 %collective-permute-start.10 = (bf16[16,2048]{1,0:T(8,128)(2,1)S(1)}, bf16[16,2048]{1,0:T(8,128)(2,1)S(1)}, u32[]{:S(2)}, u32[]{:S(2)}) collective-permute-start(bf16[16,2048]{1,0:T(8,128)(2,1)S(1)} %get-tuple-element.89), channel_id=1, source_target_pairs={{24,2},{25,3},{26,4},{27,5},{28,6},{29,7},{30,0},{31,1},{0,10},{1,... | collective-permute-start | bytes 196616 | tf_op jit(solution)/shard_map/ppermute | solution.py:111
  5.8 8.6 %collective-permute-start.11 = (bf16[16,2048]{1,0:T(8,128)(2,1)S(1)}, bf16[16,2048]{1,0:T(8,128)(2,1)S(1)}, u32[]{:S(2)}, u32[]{:S(2)}) collective-permute-start(bf16[16,2048]{1,0:T(8,128)(2,1)S(1)} %get-tuple-element.89), channel_id=1, source_target_pairs={{24,4},{25,5},{26,6},{27,7},{28,0},{29,1},{30,2},{31,3},{0,12},{1,... | collective-permute-start | bytes 196616 | tf_op jit(solution)/shard_map/ppermute | solution.py:111
  11.0 9.6 %all-to-all-start = ((f32[8,1,128]{2,1,0:T(1,128)}), f32[8,1,128]{2,1,0:T(1,128)S(1)}, u32[]{:S(2)}, u32[]{:S(2)}) async-start(f32[8,1,128]{2,1,0:T(1,128)} %reshape.193), calls=%async_computation | async-start | bytes 8192 | tf_op jit(solution)/shard_map/all_to_all | solution.py:98
  15.0 8.2 %collective-permute-start.13 = (bf16[64,2048]{1,0:T(8,128)(2,1)S(1)}, bf16[64,2048]{1,0:T(8,128)(2,1)S(1)}, u32[]{:S(2)}, u32[]{:S(2)}) collective-permute-start(bf16[64,2048]{1,0:T(8,128)(2,1)S(1)} %constant_dynamic-update-slice_fusion.4.own_ref), channel_id=1, source_target_pairs={{0,1},{1,0},{2,3},{3,2},{4,5},{5,4},{6,7},{7,6},{8,9},{9,8},{10,11... | collective-permute-start | bytes 786440 | tf_op jit(solution)/shard_map/ppermute | solution.py:114
  54.4 8.1 %collective-permute-start.29 = (bf16[16,2048]{1,0:T(8,128)(2,1)S(1)}, bf16[16,2048]{1,0:T(8,128)(2,1)S(1)}, u32[]{:S(2)}, u32[]{:S(2)}) collective-permute-start(bf16[16,2048]{1,0:T(8,128)(2,1)S(1)} %get-tuple-element.81), channel_id=1, source_target_pairs={{24,4},{25,5},{26,6},{27,7},{28,0},{29,1},{30,2},{31,3},{0,12},{1,... | collective-permute-start | bytes 196616 | tf_op jit(solution)/shard_map/ppermute | solution.py:111
  63.1 8.3 %collective-permute-start.31 = (bf16[64,2048]{1,0:T(8,128)(2,1)S(1)}, bf16[64,2048]{1,0:T(8,128)(2,1)}, u32[]{:S(2)}, u32[]{:S(2)}) collective-permute-start(bf16[64,2048]{1,0:T(8,128)(2,1)S(1)} %constant_dynamic-update-slice_fusion.12.own_ref), channel_id=1, source_target_pairs={{0,1},{1,0},{2,3},{3,2},{4,5},{5,4},{6,7},{7,6},{8,9},{9,8},{10,11... | collective-permute-start | bytes 786440 | tf_op jit(solution)/shard_map/ppermute | solution.py:114
  98.9 8.4 %collective-permute-start.47 = (bf16[16,2048]{1,0:T(8,128)(2,1)S(1)}, bf16[16,2048]{1,0:T(8,128)(2,1)S(1)}, u32[]{:S(2)}, u32[]{:S(2)}) collective-permute-start(bf16[16,2048]{1,0:T(8,128)(2,1)S(1)} %get-tuple-element.77), channel_id=1, source_target_pairs={{24,4},{25,5},{26,6},{27,7},{28,0},{29,1},{30,2},{31,3},{0,12},{1,... | collective-permute-start | bytes 196616 | tf_op jit(solution)/shard_map/ppermute | solution.py:111
  140.3 18.6 %collective-permute-start = (bf16[16,2048]{1,0:T(8,128)(2,1)}, bf16[16,2048]{1,0:T(8,128)(2,1)}, u32[]{:S(2)}, u32[]{:S(2)}) collective-permute-start(bf16[16,2048]{1,0:T(8,128)(2,1)} %get-tuple-element.90), channel_id=1, source_target_pairs={{24,0},{25,1},{26,2},{27,3},{28,4},{29,5},{30,6},{31,7},{0,8},{1,9... | collective-permute-start | bytes 196616 | tf_op jit(solution)/shard_map/ppermute | solution.py:111
  150.9 8.7 %collective-permute-start.67 = (bf16[64,2048]{1,0:T(8,128)(2,1)S(1)}, bf16[64,2048]{1,0:T(8,128)(2,1)}, u32[]{:S(2)}, u32[]{:S(2)}) collective-permute-start(bf16[64,2048]{1,0:T(8,128)(2,1)S(1)} %constant_dynamic-update-slice_fusion.28.own_ref), channel_id=1, source_target_pairs={{0,1},{1,0},{2,3},{3,2},{4,5},{5,4},{6,7},{7,6},{8,9},{9,8},{10,11... | collective-permute-start | bytes 786440 | tf_op jit(solution)/shard_map/ppermute | solution.py:114
  152.4 18.3 %collective-permute-start.1 = (bf16[16,2048]{1,0:T(8,128)(2,1)}, bf16[16,2048]{1,0:T(8,128)(2,1)}, u32[]{:S(2)}, u32[]{:S(2)}) collective-permute-start(bf16[16,2048]{1,0:T(8,128)(2,1)} %get-tuple-element.90), channel_id=1, source_target_pairs={{24,2},{25,3},{26,4},{27,5},{28,6},{29,7},{30,0},{31,1},{0,10},{1,... | collective-permute-start | bytes 196616 | tf_op jit(solution)/shard_map/ppermute | solution.py:111
  153.8 17.7 %collective-permute-start.2 = (bf16[16,2048]{1,0:T(8,128)(2,1)}, bf16[16,2048]{1,0:T(8,128)(2,1)}, u32[]{:S(2)}, u32[]{:S(2)}) collective-permute-start(bf16[16,2048]{1,0:T(8,128)(2,1)} %get-tuple-element.90), channel_id=1, source_target_pairs={{24,4},{25,5},{26,6},{27,7},{28,0},{29,1},{30,2},{31,3},{0,12},{1,... | collective-permute-start | bytes 196616 | tf_op jit(solution)/shard_map/ppermute | solution.py:111
  155.7 26.9 %collective-permute-start.3 = (bf16[16,2048]{1,0:T(8,128)(2,1)}, bf16[16,2048]{1,0:T(8,128)(2,1)}, u32[]{:S(2)}, u32[]{:S(2)}) collective-permute-start(bf16[16,2048]{1,0:T(8,128)(2,1)} %get-tuple-element.90), channel_id=1, source_target_pairs={{24,6},{25,7},{26,0},{27,1},{28,2},{29,3},{30,4},{31,5},{0,14},{1,... | collective-permute-start | bytes 196616 | tf_op jit(solution)/shard_map/ppermute | solution.py:111
  169.4 9.2 %collective-permute-start.68 = (bf16[64,2048]{1,0:T(8,128)(2,1)S(1)}, bf16[64,2048]{1,0:T(8,128)(2,1)S(1)}, u32[]{:S(2)}, u32[]{:S(2)}) collective-permute-start(bf16[64,2048]{1,0:T(8,128)(2,1)S(1)} %get-tuple-element.48), channel_id=1, source_target_pairs={{0,1},{1,0},{2,3},{3,2},{4,5},{5,4},{6,7},{7,6},{8,9},{9,8},{10,11... | collective-permute-start | bytes 786440 | tf_op jit(solution)/shard_map/ppermute | solution.py:114
  189.1 10.7 %collective-permute-start.81 = (bf16[16,2048]{1,0:T(8,128)(2,1)S(1)}, bf16[16,2048]{1,0:T(8,128)(2,1)S(1)}, u32[]{:S(2)}, u32[]{:S(2)}) collective-permute-start(bf16[16,2048]{1,0:T(8,128)(2,1)S(1)} %get-tuple-element.69), channel_id=1, source_target_pairs={{24,0},{25,1},{26,2},{27,3},{28,4},{29,5},{30,6},{31,7},{0,8},{1,9... | collective-permute-start | bytes 196616 | tf_op jit(solution)/shard_map/ppermute | solution.py:111
  195.4 9.8 %collective-permute-start.5 = (bf16[64,2048]{1,0:T(8,128)(2,1)S(1)}, bf16[64,2048]{1,0:T(8,128)(2,1)S(1)}, u32[]{:S(2)}, u32[]{:S(2)}) collective-permute-start(bf16[64,2048]{1,0:T(8,128)(2,1)S(1)} %get-tuple-element.34), channel_id=1, source_target_pairs={{0,1},{1,0},{2,3},{3,2},{4,5},{5,4},{6,7},{7,6},{8,9},{9,8},{10,11... | collective-permute-start | bytes 786440 | tf_op jit(solution)/shard_map/ppermute | solution.py:114
  196.3 8.0 %collective-permute-start.83 = (bf16[16,2048]{1,0:T(8,128)(2,1)S(1)}, bf16[16,2048]{1,0:T(8,128)(2,1)S(1)}, u32[]{:S(2)}, u32[]{:S(2)}) collective-permute-start(bf16[16,2048]{1,0:T(8,128)(2,1)S(1)} %get-tuple-element.69), channel_id=1, source_target_pairs={{24,4},{25,5},{26,6},{27,7},{28,0},{29,1},{30,2},{31,3},{0,12},{1,... | collective-permute-start | bytes 196616 | tf_op jit(solution)/shard_map/ppermute | solution.py:111
  204.3 8.0 %collective-permute-start.85 = (bf16[64,2048]{1,0:T(8,128)(2,1)S(1)}, bf16[64,2048]{1,0:T(8,128)(2,1)S(1)}, u32[]{:S(2)}, u32[]{:S(2)}) collective-permute-start(bf16[64,2048]{1,0:T(8,128)(2,1)S(1)} %constant_dynamic-update-slice_fusion.36.own_ref), channel_id=1, source_target_pairs={{0,1},{1,0},{2,3},{3,2},{4,5},{5,4},{6,7},{7,6},{8,9},{9,8},{10,11... | collective-permute-start | bytes 786440 | tf_op jit(solution)/shard_map/ppermute | solution.py:114
  216.4 7.9 %collective-permute-start.86 = (bf16[64,2048]{1,0:T(8,128)(2,1)S(1)}, bf16[64,2048]{1,0:T(8,128)(2,1)S(1)}, u32[]{:S(2)}, u32[]{:S(2)}) collective-permute-start(bf16[64,2048]{1,0:T(8,128)(2,1)S(1)} %get-tuple-element.52), channel_id=1, source_target_pairs={{0,1},{1,0},{2,3},{3,2},{4,5},{5,4},{6,7},{7,6},{8,9},{9,8},{10,11... | collective-permute-start | bytes 786440 | tf_op jit(solution)/shard_map/ppermute | solution.py:114
  218.1 9.1 %collective-permute-start.8 = (bf16[16,2048]{1,0:T(8,128)(2,1)S(1)}, bf16[16,2048]{1,0:T(8,128)(2,1)S(1)}, u32[]{:S(2)}, u32[]{:S(2)}) collective-permute-start(bf16[16,2048]{1,0:T(8,128)(2,1)S(1)} %get-tuple-element.131), channel_id=1, source_target_pairs={{0,2},{1,3},{2,4},{3,5},{4,6},{5,7},{6,0},{7,1},{8,10},{9,11},{10,... | collective-permute-start | bytes 196616 | tf_op jit(solution)/shard_map/ppermute | solution.py:111
  220.0 8.3 %collective-permute-start.7 = (bf16[16,2048]{1,0:T(8,128)(2,1)S(1)}, bf16[16,2048]{1,0:T(8,128)(2,1)S(1)}, u32[]{:S(2)}, u32[]{:S(2)}) collective-permute-start(bf16[16,2048]{1,0:T(8,128)(2,1)S(1)} %get-tuple-element.132), channel_id=1, source_target_pairs={{0,4},{1,5},{2,6},{3,7},{4,0},{5,1},{6,2},{7,3},{8,12},{9,13},{10,... | collective-permute-start | bytes 196616 | tf_op jit(solution)/shard_map/ppermute | solution.py:111
  235.9 8.4 %collective-permute-start.101 = (bf16[16,2048]{1,0:T(8,128)(2,1)S(1)}, bf16[16,2048]{1,0:T(8,128)(2,1)S(1)}, u32[]{:S(2)}, u32[]{:S(2)}) collective-permute-start(bf16[16,2048]{1,0:T(8,128)(2,1)S(1)} %get-tuple-element.65), channel_id=1, source_target_pairs={{24,4},{25,5},{26,6},{27,7},{28,0},{29,1},{30,2},{31,3},{0,12},{1,... | collective-permute-start | bytes 196616 | tf_op jit(solution)/shard_map/ppermute | solution.py:111
  237.3 9.3 %collective-permute-start.102 = (bf16[16,2048]{1,0:T(8,128)(2,1)S(1)}, bf16[16,2048]{1,0:T(8,128)(2,1)S(1)}, u32[]{:S(2)}, u32[]{:S(2)}) collective-permute-start(bf16[16,2048]{1,0:T(8,128)(2,1)S(1)} %get-tuple-element.65), channel_id=1, source_target_pairs={{24,6},{25,7},{26,0},{27,1},{28,2},{29,3},{30,4},{31,5},{0,14},{1,... | collective-permute-start | bytes 196616 | tf_op jit(solution)/shard_map/ppermute | solution.py:111
  238.6 9.6 %collective-permute-start.18 = (bf16[16,2048]{1,0:T(8,128)(2,1)}, bf16[16,2048]{1,0:T(8,128)(2,1)S(1)}, u32[]{:S(2)}, u32[]{:S(2)}) collective-permute-start(bf16[16,2048]{1,0:T(8,128)(2,1)} %get-tuple-element.87), channel_id=1, source_target_pairs={{24,0},{25,1},{26,2},{27,3},{28,4},{29,5},{30,6},{31,7},{0,8},{1,9... | collective-permute-start | bytes 196616 | tf_op jit(solution)/shard_map/ppermute | solution.py:111
  239.5 8.8 %collective-permute-start.19 = (bf16[16,2048]{1,0:T(8,128)(2,1)}, bf16[16,2048]{1,0:T(8,128)(2,1)S(1)}, u32[]{:S(2)}, u32[]{:S(2)}) collective-permute-start(bf16[16,2048]{1,0:T(8,128)(2,1)} %get-tuple-element.87), channel_id=1, source_target_pairs={{24,2},{25,3},{26,4},{27,5},{28,6},{29,7},{30,0},{31,1},{0,10},{1,... | collective-permute-start | bytes 196616 | tf_op jit(solution)/shard_map/ppermute | solution.py:111
  240.8 9.2 %collective-permute-start.20 = (bf16[16,2048]{1,0:T(8,128)(2,1)}, bf16[16,2048]{1,0:T(8,128)(2,1)S(1)}, u32[]{:S(2)}, u32[]{:S(2)}) collective-permute-start(bf16[16,2048]{1,0:T(8,128)(2,1)} %get-tuple-element.87), channel_id=1, source_target_pairs={{24,4},{25,5},{26,6},{27,7},{28,0},{29,1},{30,2},{31,3},{0,12},{1,... | collective-permute-start | bytes 196616 | tf_op jit(solution)/shard_map/ppermute | solution.py:111
  246.6 8.6 %collective-permute-start.103 = (bf16[64,2048]{1,0:T(8,128)(2,1)S(1)}, bf16[64,2048]{1,0:T(8,128)(2,1)S(1)}, u32[]{:S(2)}, u32[]{:S(2)}) collective-permute-start(bf16[64,2048]{1,0:T(8,128)(2,1)S(1)} %constant_dynamic-update-slice_fusion.44.own_ref), channel_id=1, source_target_pairs={{0,1},{1,0},{2,3},{3,2},{4,5},{5,4},{6,7},{7,6},{8,9},{9,8},{10,11... | collective-permute-start | bytes 786440 | tf_op jit(solution)/shard_map/ppermute | solution.py:114
  250.7 15.8 %collective-permute-start.22 = (bf16[64,2048]{1,0:T(8,128)(2,1)S(1)}, bf16[64,2048]{1,0:T(8,128)(2,1)}, u32[]{:S(2)}, u32[]{:S(2)}) collective-permute-start(bf16[64,2048]{1,0:T(8,128)(2,1)S(1)} %constant_dynamic-update-slice_fusion.8.own_ref), channel_id=1, source_target_pairs={{0,1},{1,0},{2,3},{3,2},{4,5},{5,4},{6,7},{7,6},{8,9},{9,8},{10,11... | collective-permute-start | bytes 786440 | tf_op jit(solution)/shard_map/ppermute | solution.py:114
  264.5 11.1 %collective-permute-start.104 = (bf16[64,2048]{1,0:T(8,128)(2,1)}, bf16[64,2048]{1,0:T(8,128)(2,1)}, u32[]{:S(2)}, u32[]{:S(2)}) collective-permute-start(bf16[64,2048]{1,0:T(8,128)(2,1)} %get-tuple-element.56), channel_id=1, source_target_pairs={{0,1},{1,0},{2,3},{3,2},{4,5},{5,4},{6,7},{7,6},{8,9},{9,8},{10,11... | collective-permute-start | bytes 786440 | tf_op jit(solution)/shard_map/ppermute | solution.py:114
  275.4 8.9 %collective-permute-start.23 = (bf16[64,2048]{1,0:T(8,128)(2,1)S(1)}, bf16[64,2048]{1,0:T(8,128)(2,1)S(1)}, u32[]{:S(2)}, u32[]{:S(2)}) collective-permute-start(bf16[64,2048]{1,0:T(8,128)(2,1)S(1)} %get-tuple-element.38), channel_id=1, source_target_pairs={{0,1},{1,0},{2,3},{3,2},{4,5},{5,4},{6,7},{7,6},{8,9},{9,8},{10,11... | collective-permute-start | bytes 786440 | tf_op jit(solution)/shard_map/ppermute | solution.py:114
  276.7 8.3 %collective-permute-start.107 = (bf16[16,2048]{1,0:T(8,128)(2,1)S(1)}, bf16[16,2048]{1,0:T(8,128)(2,1)S(1)}, u32[]{:S(2)}, u32[]{:S(2)}) collective-permute-start(bf16[16,2048]{1,0:T(8,128)(2,1)S(1)} %get-tuple-element.98), channel_id=1, source_target_pairs={{0,2},{1,3},{2,4},{3,5},{4,6},{5,7},{6,0},{7,1},{8,10},{9,11},{10,... | collective-permute-start | bytes 196616 | tf_op jit(solution)/shard_map/ppermute | solution.py:111
  279.8 8.5 %collective-permute-start.106 = (bf16[16,2048]{1,0:T(8,128)(2,1)S(1)}, bf16[16,2048]{1,0:T(8,128)(2,1)S(1)}, u32[]{:S(2)}, u32[]{:S(2)}) collective-permute-start(bf16[16,2048]{1,0:T(8,128)(2,1)S(1)} %get-tuple-element.99), channel_id=1, source_target_pairs={{0,4},{1,5},{2,6},{3,7},{4,0},{5,1},{6,2},{7,3},{8,12},{9,13},{10,... | collective-permute-start | bytes 196616 | tf_op jit(solution)/shard_map/ppermute | solution.py:111
  279.8 8.5 %collective-permute-start.105 = (bf16[16,2048]{1,0:T(8,128)(2,1)S(1)}, bf16[16,2048]{1,0:T(8,128)(2,1)S(1)}, u32[]{:S(2)}, u32[]{:S(2)}) collective-permute-start(bf16[16,2048]{1,0:T(8,128)(2,1)S(1)} %get-tuple-element.97), channel_id=1, source_target_pairs={{0,6},{1,7},{2,0},{3,1},{4,2},{5,3},{6,4},{7,5},{8,14},{9,15},{10,... | collective-permute-start | bytes 196616 | tf_op jit(solution)/shard_map/ppermute | solution.py:111
  284.7 8.1 %collective-permute-start.25 = (bf16[16,2048]{1,0:T(8,128)(2,1)S(1)}, bf16[16,2048]{1,0:T(8,128)(2,1)S(1)}, u32[]{:S(2)}, u32[]{:S(2)}) collective-permute-start(bf16[16,2048]{1,0:T(8,128)(2,1)S(1)} %get-tuple-element.126), channel_id=1, source_target_pairs={{0,4},{1,5},{2,6},{3,7},{4,0},{5,1},{6,2},{7,3},{8,12},{9,13},{10,... | collective-permute-start | bytes 196616 | tf_op jit(solution)/shard_map/ppermute | solution.py:111
  304.6 8.2 %collective-permute-start.40 = (bf16[64,2048]{1,0:T(8,128)(2,1)S(1)}, bf16[64,2048]{1,0:T(8,128)(2,1)}, u32[]{:S(2)}, u32[]{:S(2)}) collective-permute-start(bf16[64,2048]{1,0:T(8,128)(2,1)S(1)} %constant_dynamic-update-slice_fusion.16.own_ref), channel_id=1, source_target_pairs={{0,1},{1,0},{2,3},{3,2},{4,5},{5,4},{6,7},{7,6},{8,9},{9,8},{10,11... | collective-permute-start | bytes 786440 | tf_op jit(solution)/shard_map/ppermute | solution.py:114
  341.8 24.9 %collective-permute-start.117 = (bf16[16,2048]{1,0:T(8,128)(2,1)}, bf16[16,2048]{1,0:T(8,128)(2,1)S(1)}, u32[]{:S(2)}, u32[]{:S(2)}) collective-permute-start(bf16[16,2048]{1,0:T(8,128)(2,1)} %get-tuple-element.61), channel_id=1, source_target_pairs={{24,0},{25,1},{26,2},{27,3},{28,4},{29,5},{30,6},{31,7},{0,8},{1,9... | collective-permute-start | bytes 196616 | tf_op jit(solution)/shard_map/ppermute | solution.py:111
  342.0 39.8 %collective-permute-start.118 = (bf16[16,2048]{1,0:T(8,128)(2,1)}, bf16[16,2048]{1,0:T(8,128)(2,1)S(1)}, u32[]{:S(2)}, u32[]{:S(2)}) collective-permute-start(bf16[16,2048]{1,0:T(8,128)(2,1)} %get-tuple-element.61), channel_id=1, source_target_pairs={{24,2},{25,3},{26,4},{27,5},{28,6},{29,7},{30,0},{31,1},{0,10},{1,... | collective-permute-start | bytes 196616 | tf_op jit(solution)/shard_map/ppermute | solution.py:111
  342.8 39.1 %collective-permute-start.119 = (bf16[16,2048]{1,0:T(8,128)(2,1)}, bf16[16,2048]{1,0:T(8,128)(2,1)S(1)}, u32[]{:S(2)}, u32[]{:S(2)}) collective-permute-start(bf16[16,2048]{1,0:T(8,128)(2,1)} %get-tuple-element.61), channel_id=1, source_target_pairs={{24,4},{25,5},{26,6},{27,7},{28,0},{29,1},{30,2},{31,3},{0,12},{1,... | collective-permute-start | bytes 196616 | tf_op jit(solution)/shard_map/ppermute | solution.py:111
  345.9 47.6 %collective-permute-start.120 = (bf16[16,2048]{1,0:T(8,128)(2,1)}, bf16[16,2048]{1,0:T(8,128)(2,1)S(1)}, u32[]{:S(2)}, u32[]{:S(2)}) collective-permute-start(bf16[16,2048]{1,0:T(8,128)(2,1)} %get-tuple-element.61), channel_id=1, source_target_pairs={{24,6},{25,7},{26,0},{27,1},{28,2},{29,3},{30,4},{31,5},{0,14},{1,... | collective-permute-start | bytes 196616 | tf_op jit(solution)/shard_map/ppermute | solution.py:111
  396.4 11.7 %collective-permute-start.72 = (bf16[16,2048]{1,0:T(8,128)(2,1)S(1)}, bf16[16,2048]{1,0:T(8,128)(2,1)S(1)}, u32[]{:S(2)}, u32[]{:S(2)}) collective-permute-start(bf16[16,2048]{1,0:T(8,128)(2,1)S(1)} %get-tuple-element.71), channel_id=1, source_target_pairs={{24,0},{25,1},{26,2},{27,3},{28,4},{29,5},{30,6},{31,7},{0,8},{1,9... | collective-permute-start | bytes 196616 | tf_op jit(solution)/shard_map/ppermute | solution.py:111
  404.1 21.5 %collective-permute-start.122 = (bf16[64,2048]{1,0:T(8,128)(2,1)S(1)}, bf16[64,2048]{1,0:T(8,128)(2,1)S(1)}, u32[]{:S(2)}, u32[]{:S(2)}) collective-permute-start(bf16[64,2048]{1,0:T(8,128)(2,1)S(1)} %get-tuple-element.60), channel_id=1, source_target_pairs={{0,1},{1,0},{2,3},{3,2},{4,5},{5,4},{6,7},{7,6},{8,9},{9,8},{10,11... | collective-permute-start | bytes 786440 | tf_op jit(solution)/shard_map/ppermute | solution.py:114
  404.6 7.9 %collective-permute-start.74 = (bf16[16,2048]{1,0:T(8,128)(2,1)S(1)}, bf16[16,2048]{1,0:T(8,128)(2,1)S(1)}, u32[]{:S(2)}, u32[]{:S(2)}) collective-permute-start(bf16[16,2048]{1,0:T(8,128)(2,1)S(1)} %get-tuple-element.71), channel_id=1, source_target_pairs={{24,4},{25,5},{26,6},{27,7},{28,0},{29,1},{30,2},{31,3},{0,12},{1,... | collective-permute-start | bytes 196616 | tf_op jit(solution)/shard_map/ppermute | solution.py:111
  412.5 7.9 %collective-permute-start.76 = (bf16[64,2048]{1,0:T(8,128)(2,1)S(1)}, bf16[64,2048]{1,0:T(8,128)(2,1)S(1)}, u32[]{:S(2)}, u32[]{:S(2)}) collective-permute-start(bf16[64,2048]{1,0:T(8,128)(2,1)S(1)} %constant_dynamic-update-slice_fusion.32.own_ref), channel_id=1, source_target_pairs={{0,1},{1,0},{2,3},{3,2},{4,5},{5,4},{6,7},{7,6},{8,9},{9,8},{10,11... | collective-permute-start | bytes 786440 | tf_op jit(solution)/shard_map/ppermute | solution.py:114
  433.1 8.8 %collective-permute-start.79 = (bf16[16,2048]{1,0:T(8,128)(2,1)S(1)}, bf16[16,2048]{1,0:T(8,128)(2,1)S(1)}, u32[]{:S(2)}, u32[]{:S(2)}) collective-permute-start(bf16[16,2048]{1,0:T(8,128)(2,1)S(1)} %get-tuple-element.108), channel_id=1, source_target_pairs={{0,4},{1,5},{2,6},{3,7},{4,0},{5,1},{6,2},{7,3},{8,12},{9,13},{10,... | collective-permute-start | bytes 196616 | tf_op jit(solution)/shard_map/ppermute | solution.py:111
  435.5 85.3 %collective-permute-start.125 = (bf16[16,2048]{1,0:T(8,128)(2,1)S(1)}, bf16[16,2048]{1,0:T(8,128)(2,1)S(1)}, u32[]{:S(2)}, u32[]{:S(2)}) collective-permute-start(bf16[16,2048]{1,0:T(8,128)(2,1)S(1)} %get-tuple-element.92), channel_id=1, source_target_pairs={{0,2},{1,3},{2,4},{3,5},{4,6},{5,7},{6,0},{7,1},{8,10},{9,11},{10,... | collective-permute-start | bytes 196616 | tf_op jit(solution)/shard_map/ppermute | solution.py:111
  437.5 83.3 %collective-permute-start.124 = (bf16[16,2048]{1,0:T(8,128)(2,1)S(1)}, bf16[16,2048]{1,0:T(8,128)(2,1)S(1)}, u32[]{:S(2)}, u32[]{:S(2)}) collective-permute-start(bf16[16,2048]{1,0:T(8,128)(2,1)S(1)} %get-tuple-element.93), channel_id=1, source_target_pairs={{0,4},{1,5},{2,6},{3,7},{4,0},{5,1},{6,2},{7,3},{8,12},{9,13},{10,... | collective-permute-start | bytes 196616 | tf_op jit(solution)/shard_map/ppermute | solution.py:111
  454.3 8.3 %collective-permute-start.94 = (bf16[64,2048]{1,0:T(8,128)(2,1)S(1)}, bf16[64,2048]{1,0:T(8,128)(2,1)S(1)}, u32[]{:S(2)}, u32[]{:S(2)}) collective-permute-start(bf16[64,2048]{1,0:T(8,128)(2,1)S(1)} %constant_dynamic-update-slice_fusion.40.own_ref), channel_id=1, source_target_pairs={{0,1},{1,0},{2,3},{3,2},{4,5},{5,4},{6,7},{7,6},{8,9},{9,8},{10,11... | collective-permute-start | bytes 786440 | tf_op jit(solution)/shard_map/ppermute | solution.py:114
  492.9 8.3 %collective-permute-start.112 = (bf16[64,2048]{1,0:T(8,128)(2,1)S(1)}, bf16[64,2048]{1,0:T(8,128)(2,1)S(1)}, u32[]{:S(2)}, u32[]{:S(2)}) collective-permute-start(bf16[64,2048]{1,0:T(8,128)(2,1)S(1)} %constant_dynamic-update-slice_fusion.48.own_ref), channel_id=1, source_target_pairs={{0,1},{1,0},{2,3},{3,2},{4,5},{5,4},{6,7},{7,6},{8,9},{9,8},{10,11... | collective-permute-start | bytes 786440 | tf_op jit(solution)/shard_map/ppermute | solution.py:114
  (122 other events, 899.7 us)
